TPU v7x, 32 devices: a whole 2x2x4 slice. The times are simulated.
32 devices in a mesh: dp: 8 (over z, x), row: 2 (over y), col: 2 (over core).
Axes of the slice: x: 2, y: 2, z: 4, core: 2. Of those that a mesh axis runs over, the one named last changes fastest.
Arguments:
- tokens: bfloat16 [2048, 1024], P(('dp', 'row'), 'col'), may hold values from -40 to 40
- cotangent: bfloat16 [2048, 1024], P(('dp', 'row'), 'col'), may hold values from -6 to 6
- w_query: bfloat16 [1024, 2048], P('col', 'row'), may hold values from -0.1875 to 0.1875
- key_weight: bfloat16 [1024, 1024], P('col', 'row'), may hold values from -0.1875 to 0.1875
- value_weight: bfloat16 [1024, 1024], P('col', 'row'), may hold values from -0.1875 to 0.1875
- w_output: bfloat16 [2048, 1024], P('row', 'col'), may hold values from -1 to 1
- w_gate: bfloat16 [1024, 3072], P('col', 'row'), may hold values from -0.1875 to 0.1875
- w_up: bfloat16 [1024, 3072], P('col', 'row'), may hold values from -0.1875 to 0.1875
- w_down: bfloat16 [3072, 1024], P('row', 'col'), may hold values from -0.109375 to 0.109375
- gain_attn: float32 [1024], P('col'), may hold values from 0.5 to 1.5
- gain_query: float32 [128], replicated, may hold values from 0.5 to 1.5
- gain_key: float32 [128], replicated, may hold values from 0.5 to 1.5
- gain_mlp: float32 [1024], P('col'), may hold values from 0.5 to 1.5
- seq_lengths: int32 [24], replicated, may hold values from 1 to 254, as said below
- seq_groups: int32 [24], replicated, may hold values from 0 to 7, as said below
Outputs:
- mixed: bfloat16 [2048, 1024], P(('dp', 'row'), 'col')
- input_grad: float32 [2048, 1024], P(('dp', 'row'), 'col')
- w_query_grad: float32 [1024, 2048], P(('col', 'dp'), 'row')
- w_key_grad: float32 [1024, 1024], P(('col', 'dp'), 'row')
- w_value_grad: float32 [1024, 1024], P(('col', 'dp'), 'row')
- w_output_grad: float32 [2048, 1024], P(('row', 'dp'), 'col')
- w_gate_grad: float32 [1024, 3072], P(('col', 'dp'), 'row')
- w_up_grad: float32 [1024, 3072], P(('col', 'dp'), 'row')
- w_down_grad: float32 [3072, 1024], P(('row', 'dp'), 'col')
- gain_attn_grad: float32 [1024], P('col')
- gain_query_grad: float32 [128], replicated
- gain_key_grad: float32 [128], replicated
- gain_mlp_grad: float32 [1024], P('col')
Inputs may be any that keep to these rules, and one draw needn't show every extreme that they name: `seq_lengths`: the 3 sequences that seq_groups gives to one index of dp fill its 256 rows from the first, one after another in the order of their numbers, and total at most 256; one of them is longer than 128; in some index they total exactly 256. `seq_groups`: every index of dp holds exactly 3 sequences.
All inputs are finite; a program needn't handle non-finite values.
Results may differ from a plain program's by a relative error of at most 0.012.
Values may be sent and summed in bfloat16 or wider, within the bound.
A program may use at most 128 MiB of HBM per device.

v0:
```python
import math

import jax
import jax.numpy as jnp
from jax import lax
from jax.sharding import PartitionSpec as P

EPS = 1e-06
THETA = 1000000.0
NEGATIVE = -1e30


def layout(lengths, groups, group, slots):
    count = lengths.shape[0]
    mine = groups == group
    sizes_here = jnp.where(mine, lengths, 0)
    starts = jnp.cumsum(sizes_here) - sizes_here
    place = lax.broadcasted_iota(jnp.int32, (slots, count), 0)
    number = lax.broadcasted_iota(jnp.int32, (slots, count), 1)
    inside = mine[None, :] & (place >= starts[None, :]) & (place < (starts + sizes_here)[None, :])
    found = jnp.sum(inside.astype(jnp.int32), axis=1)
    segment = jnp.sum(jnp.where(inside, number, 0), axis=1)
    spot = lax.broadcasted_iota(jnp.int32, (slots,), 0)
    segment = jnp.where(found > 0, segment, count + spot)
    position = jnp.sum(jnp.where(inside, place - starts[None, :], 0), axis=1)
    return (segment, position)


def allowed_pairs(segment):
    slots = segment.shape[0]
    later = lax.broadcasted_iota(jnp.int32, (slots, slots), 0)
    earlier = lax.broadcasted_iota(jnp.int32, (slots, slots), 1)
    return (segment[:, None] == segment[None, :]) & (earlier <= later)


def rotate(value_rows, position):
    size = value_rows.shape[-1]
    half = size // 2
    freq = THETA ** (-(jnp.arange(half, dtype=jnp.float32) * 2.0 / size))
    angle = position.astype(jnp.float32)[:, None] * freq[None, :]
    cosine = jnp.cos(angle)[:, None, :]
    sine = jnp.sin(angle)[:, None, :]
    first = value_rows[..., :half]
    second = value_rows[..., half:]
    return jnp.concatenate(
        [first * cosine - second * sine, second * cosine + first * sine], axis=-1
    )


def rms_scale(value_rows, gain):
    return (
        value_rows
        * lax.rsqrt(jnp.mean(value_rows * value_rows, axis=-1, keepdims=True) + EPS)
        * gain
    )


def swiglu(gate, up_part):
    return jax.nn.silu(gate) * up_part


def product(left, right):
    return jnp.dot(left, right, preferred_element_type=jnp.float32)


def contract_rows(left, right):
    return lax.dot_general(
        left, right, (((0,), (0,)), ((), ())), preferred_element_type=jnp.float32
    )


def contract_cols(left, right):
    return lax.dot_general(
        left, right, (((1,), (1,)), ((), ())), preferred_element_type=jnp.float32
    )


def gather_tokens(local):
    return lax.all_gather(local, "row", axis=0, tiled=True)


def gather_units(local):
    return lax.all_gather(local, "col", axis=1, tiled=True)


def sum_tokens(partial_value):
    return lax.psum_scatter(partial_value, "row", scatter_dimension=0, tiled=True)


def sum_units(partial_value):
    return lax.psum_scatter(partial_value, "col", scatter_dimension=1, tiled=True)


def width_sum(vector):
    return lax.psum(vector, "col")


def inverse_rms(value_rows, width):
    total = width_sum(jnp.sum(value_rows * value_rows, axis=1))
    return lax.rsqrt(total / width + EPS)[:, None]


def norm_back(value_rows, inverse, gain, grad, width):
    scaled = grad * gain
    inner = width_sum(jnp.sum(scaled * value_rows, axis=1))
    result = inverse * scaled - value_rows * inverse**3 * (inner / width)[:, None]
    gain_part = jnp.sum(grad * value_rows * inverse, axis=0)
    return (result, gain_part)


def attend(query_low, key_low, value_low, allowed, scale):
    token_rows, key_heads, head_dim = key_low.shape
    rank_share = query_low.shape[1] // key_heads
    grouped = query_low.reshape(token_rows, key_heads, rank_share, head_dim)
    raw = jnp.einsum("qhgd,khd->hgqk", grouped, key_low, preferred_element_type=jnp.float32)
    scores = jnp.where(allowed, raw * scale, NEGATIVE)
    top = jnp.max(scores, axis=-1, keepdims=True)
    exponent = jnp.exp(scores - top)
    total = jnp.sum(exponent, axis=-1, keepdims=True)
    probs = exponent / total
    attended = jnp.einsum(
        "hgqk,khd->qhgd", probs.astype(jnp.bfloat16), value_low, preferred_element_type=jnp.float32
    )
    return (attended.reshape(token_rows, key_heads * rank_share, head_dim), top + jnp.log(total))


def attend_back(query_low, key_low, value_low, attended_grad, lse_kept, allowed, scale):
    token_rows, key_heads, head_dim = key_low.shape
    rank_share = query_low.shape[1] // key_heads
    grouped = query_low.reshape(token_rows, key_heads, rank_share, head_dim)
    grad_grouped = attended_grad.reshape(token_rows, key_heads, rank_share, head_dim)
    raw = jnp.einsum("qhgd,khd->hgqk", grouped, key_low, preferred_element_type=jnp.float32)
    scores = jnp.where(allowed, raw * scale, NEGATIVE)
    probs = jnp.exp(scores - lse_kept)
    prob_grad = jnp.einsum(
        "qhgd,khd->hgqk", grad_grouped, value_low, preferred_element_type=jnp.float32
    )
    inner = jnp.sum(probs * prob_grad, axis=-1, keepdims=True)
    score_grad = (probs * (prob_grad - inner)).astype(jnp.bfloat16)
    query_grad = (
        jnp.einsum("hgqk,khd->qhgd", score_grad, key_low, preferred_element_type=jnp.float32)
        * scale
    )
    key_grad = (
        jnp.einsum("hgqk,qhgd->khd", score_grad, grouped, preferred_element_type=jnp.float32)
        * scale
    )
    value_grad = jnp.einsum(
        "hgqk,qhgd->khd",
        probs.astype(jnp.bfloat16),
        grad_grouped,
        preferred_element_type=jnp.float32,
    )
    return (
        query_grad.reshape(token_rows, key_heads * rank_share, head_dim),
        key_grad,
        value_grad.astype(jnp.bfloat16),
    )


def shards(
    tokens,
    cotangent,
    w_query,
    key_weight,
    value_weight,
    w_output,
    w_gate,
    w_up,
    w_down,
    gain_attn,
    gain_query,
    gain_key,
    gain_mlp,
    seq_lengths,
    seq_groups,
):
    half_rows, columns = tokens.shape
    width = columns * lax.axis_size("col")
    group_rows = half_rows * lax.axis_size("row")
    head_dim = gain_query.shape[0]
    segment, position = layout(seq_lengths, seq_groups, lax.axis_index("dp"), group_rows)
    allowed = allowed_pairs(segment)
    scale = 1.0 / math.sqrt(head_dim)
    inputs = tokens.astype(jnp.float32)
    inverse_attn = inverse_rms(inputs, width)
    normed_attn = (inputs * inverse_attn * gain_attn).astype(jnp.bfloat16)
    normed_whole = gather_tokens(normed_attn)
    query_sum, key_sum, value_sum = (
        lax.psum_scatter(product(normed_whole, w_query), "col", scatter_dimension=1, tiled=True),
        lax.psum_scatter(product(normed_whole, key_weight), "col", scatter_dimension=1, tiled=True),
        lax.psum_scatter(
            product(normed_whole, value_weight), "col", scatter_dimension=1, tiled=True
        ),
    )
    query_heads = query_sum.shape[1] // head_dim
    key_heads = key_sum.shape[1] // head_dim

    def turn(value_rows, gain):
        return rotate(rms_scale(value_rows, gain), position)

    query_rot, query_pull = jax.vjp(
        turn, query_sum.reshape(group_rows, query_heads, head_dim), gain_query
    )
    key_rot, key_pull = jax.vjp(turn, key_sum.reshape(group_rows, key_heads, head_dim), gain_key)
    query_low = query_rot.astype(jnp.bfloat16)
    key_low = key_rot.astype(jnp.bfloat16)
    value_low = value_sum.astype(jnp.bfloat16).reshape(group_rows, key_heads, head_dim)
    attended, lse_kept = attend(query_low, key_low, value_low, allowed, scale)
    attended_low = attended.reshape(group_rows, query_heads * head_dim).astype(jnp.bfloat16)
    attended_whole = gather_units(attended_low)
    hidden = inputs + sum_tokens(product(attended_whole, w_output))
    inverse_mlp = inverse_rms(hidden, width)
    normed_mlp = (hidden * inverse_mlp * gain_mlp).astype(jnp.bfloat16)
    mlp_whole = gather_tokens(normed_mlp)
    gate, up_part = (
        lax.psum_scatter(product(mlp_whole, w_gate), "col", scatter_dimension=1, tiled=True),
        lax.psum_scatter(product(mlp_whole, w_up), "col", scatter_dimension=1, tiled=True),
    )
    activated, swish_pull = jax.vjp(swiglu, gate, up_part)
    activated_low = activated.astype(jnp.bfloat16)
    activated_whole = gather_units(activated_low)
    mixed = (hidden + sum_tokens(product(activated_whole, w_down))).astype(jnp.bfloat16)
    out_grad = cotangent.astype(jnp.float32)
    out_whole = gather_tokens(cotangent)
    down_part = contract_rows(activated_whole, out_whole)
    act_grad = sum_units(contract_cols(out_whole, w_down))
    gate_grad, up_grad = swish_pull(act_grad)
    gate_whole, up_whole = (
        lax.all_gather(gate_grad.astype(jnp.bfloat16), "col", axis=1, tiled=True),
        lax.all_gather(up_grad.astype(jnp.bfloat16), "col", axis=1, tiled=True),
    )
    gate_part = contract_rows(mlp_whole, gate_whole)
    up_weight_part = contract_rows(mlp_whole, up_whole)
    normed_mlp_grad = sum_tokens(contract_cols(gate_whole, w_gate) + contract_cols(up_whole, w_up))
    mlp_norm_grad, gain_mlp_part = norm_back(hidden, inverse_mlp, gain_mlp, normed_mlp_grad, width)
    hidden_grad = out_grad + mlp_norm_grad
    hidden_whole = gather_tokens(hidden_grad.astype(jnp.bfloat16))
    output_part = contract_rows(attended_whole, hidden_whole)
    attended_grad = sum_units(contract_cols(hidden_whole, w_output)).astype(jnp.bfloat16)
    query_grad, key_grad, value_grad = attend_back(
        query_low, key_low, value_low, attended_grad, lse_kept, allowed, scale
    )
    query_pre, gain_query_part = query_pull(query_grad)
    key_pre, gain_key_part = key_pull(key_grad)
    query_pre_low = query_pre.reshape(group_rows, query_heads * head_dim).astype(jnp.bfloat16)
    key_pre_low = key_pre.reshape(group_rows, key_heads * head_dim).astype(jnp.bfloat16)
    value_grad_low = value_grad.reshape(group_rows, key_heads * head_dim)
    query_whole, key_whole, value_whole = (
        lax.all_gather(query_pre_low, "col", axis=1, tiled=True),
        lax.all_gather(key_pre_low, "col", axis=1, tiled=True),
        lax.all_gather(value_grad_low, "col", axis=1, tiled=True),
    )
    query_part = contract_rows(normed_whole, query_whole)
    key_part = contract_rows(normed_whole, key_whole)
    value_part = contract_rows(normed_whole, value_whole)
    normed_attn_grad = sum_tokens(
        contract_cols(query_whole, w_query)
        + contract_cols(key_whole, key_weight)
        + contract_cols(value_whole, value_weight)
    )
    attn_norm_grad, gain_attn_part = norm_back(
        inputs, inverse_attn, gain_attn, normed_attn_grad, width
    )
    input_grad = hidden_grad + attn_norm_grad
    col_start = lax.axis_index("col") * columns
    attn_full = lax.dynamic_update_slice(
        jnp.zeros((width,), jnp.float32), gain_attn_part, (col_start,)
    )
    mlp_full = lax.dynamic_update_slice(
        jnp.zeros((width,), jnp.float32), gain_mlp_part, (col_start,)
    )
    attn_total, query_total, key_total, mlp_total = lax.psum(
        (attn_full, gain_query_part, gain_key_part, mlp_full), ("dp", "row", "col")
    )
    gain_attn_grad = lax.dynamic_slice(attn_total, (col_start,), (columns,))
    gain_mlp_grad = lax.dynamic_slice(mlp_total, (col_start,), (columns,))
    query_total_w, key_total_w, value_total_w, output_total_w, gate_total, up_total, down_total = (
        lax.psum_scatter(query_part, "dp", scatter_dimension=0, tiled=True),
        lax.psum_scatter(key_part, "dp", scatter_dimension=0, tiled=True),
        lax.psum_scatter(value_part, "dp", scatter_dimension=0, tiled=True),
        lax.psum_scatter(output_part, "dp", scatter_dimension=0, tiled=True),
        lax.psum_scatter(gate_part, "dp", scatter_dimension=0, tiled=True),
        lax.psum_scatter(up_weight_part, "dp", scatter_dimension=0, tiled=True),
        lax.psum_scatter(down_part, "dp", scatter_dimension=0, tiled=True),
    )
    return (
        mixed,
        input_grad,
        query_total_w,
        key_total_w,
        value_total_w,
        output_total_w,
        gate_total,
        up_total,
        down_total,
        gain_attn_grad,
        query_total,
        key_total,
        gain_mlp_grad,
    )


def solution(mesh):
    in_specs = (
        P(("dp", "row"), "col"),
        P(("dp", "row"), "col"),
        P("col", "row"),
        P("col", "row"),
        P("col", "row"),
        P("row", "col"),
        P("col", "row"),
        P("col", "row"),
        P("row", "col"),
        P("col"),
        P(),
        P(),
        P("col"),
        P(),
        P(),
    )
    out_specs = (
        P(("dp", "row"), "col"),
        P(("dp", "row"), "col"),
        P(("col", "dp"), "row"),
        P(("col", "dp"), "row"),
        P(("col", "dp"), "row"),
        P(("row", "dp"), "col"),
        P(("col", "dp"), "row"),
        P(("col", "dp"), "row"),
        P(("row", "dp"), "col"),
        P("col"),
        P(),
        P(),
        P("col"),
    )
    return jax.shard_map(shards, mesh=mesh, in_specs=in_specs, out_specs=out_specs, check_vma=False)
```

profile of v0, /device:TPU:0, one launch (start us, length us, event | category | flops | bytes accessed | tf_op | source)
XLA Modules:
  0.0 744.3 jit_solution(15776466486343703121)
XLA Ops:
  13.1 7.3 all_gather.33
  27.2 5.1 reduce-scatter.21.cloned.1.call-done
  33.9 9.9 %reduce-scatter.19.cloned.1.call-done = f32[256,256]{1,0:T(8,128)} async-done(((f32[256,512]{1,0:T(8,128)}), f32[256,256]{1,0:T(8,128)}) %reduce-scatter.19.cloned.1.call-update) | async-done | bytes 262160 | tf_op jit(solution)/shard_map/reduce_scatter | solution.py:192
  46.5 9.3 %reduce-scatter.23.cloned.1.call-done = f32[256,512]{1,0:T(8,128)} async-done(((f32[256,1024]{1,0:T(8,128)}), f32[256,512]{1,0:T(8,128)}) %reduce-scatter.23.cloned.1.call-update) | async-done | bytes 524304 | tf_op jit(solution)/shard_map/reduce_scatter | solution.py:190
  64.8 6.6 all_gather.37
  72.2 3.2 fusion.49
  75.4 5.2 reduce-scatter.25.cloned.1.call-done
  88.7 6.2 all_gather.35
  97.4 3.2 fusion.47
  100.8 5.8 reduce-scatter.27.cloned.1.call-done
  106.6 12.5 %reduce-scatter.29.cloned.1.call-done = f32[256,768]{1,0:T(8,128)} async-done(((f32[256,1536]{1,0:T(8,128)}), f32[256,768]{1,0:T(8,128)}) %reduce-scatter.29.cloned.1.call-update) | async-done | bytes 786448 | tf_op jit(solution)/shard_map/reduce_scatter | solution.py:218
  136.9 9.5 %reduce-scatter.35.cloned.1.call-done = f32[128,512]{1,0:T(8,128)} async-done(((f32[256,512]{1,0:T(8,128)}), f32[128,512]{1,0:T(8,128)}) %reduce-scatter.35.cloned.1.call-update) | async-done | bytes 262160 | tf_op jit(solution)/shard_map/reduce_scatter | solution.py:87
  148.2 3.1 psum.58
  152.5 10.8 %reduce-scatter.31.cloned.1.call-done = f32[128,512]{1,0:T(8,128)} async-done(((f32[256,512]{1,0:T(8,128)}), f32[128,512]{1,0:T(8,128)}) %reduce-scatter.31.cloned.1.call-update) | async-done | bytes 262160 | tf_op jit(solution)/shard_map/reduce_scatter | solution.py:87
  165.4 5.9 all_gather.40
  174.4 7.8 %reduce-scatter.37.cloned.1.call-done = f32[256,512]{1,0:T(8,128)} async-done(((f32[256,1024]{1,0:T(8,128)}), f32[256,512]{1,0:T(8,128)}) %reduce-scatter.37.cloned.1.call-update) | async-done | bytes 524304 | tf_op jit(solution)/shard_map/reduce_scatter | solution.py:91
  230.1 41.3 %all-reduce.4 = (f32[1024]{0:T(1024)S(1)}, f32[128]{0:T(128)}, f32[128]{0:T(128)}, f32[1024]{0:T(1024)S(1)}) all-reduce(f32[1024]{0:T(1024)S(1)} %dynamic_update_slice.6, f32[128]{0:T(128)S(1)} %copy-done.57, f32[128]{0:T(128)S(1)} %get-tuple-element.15, ...), channel_id=1, replica_groups=mesh['dp'=8,'row'=2,'col'=2] {'dp','row','col'}, use_global_device_ids=true, to_apply=%region_38.39 | all-reduce | flops 2304 | bytes 18432 | tf_op jit(solution)/shard_map/psum | solution.py:273
  276.9 22.3 %reduce-scatter.47.cloned.1.call-done = f32[128,512]{1,0:T(8,128)} async-done(((f32[1024,512]{1,0:T(8,128)}), f32[128,512]{1,0:T(8,128)}) %reduce-scatter.47.cloned.1.call-update) | async-done | bytes 262160 | tf_op jit(solution)/shard_map/reduce_scatter | solution.py:282
  299.2 66.9 %reduce-scatter.43.cloned.1.call-done = f32[64,512]{1,0:T(8,128)} async-done(((f32[512,512]{1,0:T(8,128)}), f32[64,512]{1,0:T(8,128)}) %reduce-scatter.43.cloned.1.call-update) | async-done | bytes 131088 | tf_op jit(solution)/shard_map/reduce_scatter | solution.py:280
  366.1 66.4 %reduce-scatter.45.cloned.1.call-done = f32[64,512]{1,0:T(8,128)} async-done(((f32[512,512]{1,0:T(8,128)}), f32[64,512]{1,0:T(8,128)}) %reduce-scatter.45.cloned.1.call-update) | async-done | bytes 131088 | tf_op jit(solution)/shard_map/reduce_scatter | solution.py:281
  432.5 78.0 %reduce-scatter.49.cloned.1.call-done = f32[64,1536]{1,0:T(8,128)} async-done(((f32[512,1536]{1,0:T(8,128)}), f32[64,1536]{1,0:T(8,128)}) %reduce-scatter.49.cloned.1.call-update) | async-done | bytes 393232 | tf_op jit(solution)/shard_map/reduce_scatter | solution.py:283
  510.4 77.8 %reduce-scatter.51.cloned.1.call-done = f32[64,1536]{1,0:T(8,128)} async-done(((f32[512,1536]{1,0:T(8,128)}), f32[64,1536]{1,0:T(8,128)}) %reduce-scatter.51.cloned.1.call-update) | async-done | bytes 393232 | tf_op jit(solution)/shard_map/reduce_scatter | solution.py:284
  588.3 77.9 %reduce-scatter.53.cloned.1.call-done = f32[192,512]{1,0:T(8,128)} async-done(((f32[1536,512]{1,0:T(8,128)}), f32[192,512]{1,0:T(8,128)}) %reduce-scatter.53.cloned.1.call-update) | async-done | bytes 393232 | tf_op jit(solution)/shard_map/reduce_scatter | solution.py:285
  666.2 71.2 %reduce-scatter.41.cloned.1.call-done = f32[64,1024]{1,0:T(8,128)} async-done(((f32[512,1024]{1,0:T(8,128)}), f32[64,1024]{1,0:T(8,128)}) %reduce-scatter.41.cloned.1.call-update) | async-done | bytes 262160 | tf_op jit(solution)/shard_map/reduce_scatter | solution.py:279
  (262 shorter events, 115.8 us)
Async XLA Ops:
  7.2 88.4 %copy-start = (bf16[512,1536]{1,0:T(8,128)(2,1)S(1)}, bf16[512,1536]{1,0:T(8,128)(2,1)}, u32[]{:S(2)}) copy-start(bf16[512,1536]{1,0:T(8,128)(2,1)} %param.21) | copy-start | bytes 4718596
  7.2 25.1 %reduce-scatter.21.cloned.1.call-start = ((), (), s32[]{:S(2)}) async-start(), calls=%async_computation.19 | async-start | bytes 786432 | tf_op jit(solution)/shard_map/reduce_scatter | solution.py:191
  22.7 21.1 %reduce-scatter.19.cloned.1.call-start = ((), (), s32[]{:S(2)}) async-start(), calls=%async_computation.18 | async-start | bytes 786432 | tf_op jit(solution)/shard_map/reduce_scatter | solution.py:192
  24.0 31.8 %reduce-scatter.23.cloned.1.call-start = ((), (), s32[]{:S(2)}) async-start(), calls=%async_computation.20 | async-start | bytes 1572864 | tf_op jit(solution)/shard_map/reduce_scatter | solution.py:190
  25.4 20.0 %copy-start.52 = (f32[128]{0:T(128)S(1)}, f32[128]{0:T(128)}, u32[]{:S(2)}) copy-start(f32[128]{0:T(128)} %param.26) | copy-start | bytes 1540
  25.5 55.2 %reduce-scatter.25.cloned.1.call-start = ((), (), s32[]{:S(2)}) async-start(), calls=%async_computation.21 | async-start | bytes 786432 | tf_op jit(solution)/shard_map/reduce_scatter | solution.py:87
  27.2 30.8 %copy-start.18 = (f32[256,64]{1,0:T(8,128)}, f32[256,64]{1,0:T(8,128)S(1)}, u32[]{:S(2)}) copy-start(f32[256,64]{1,0:T(8,128)S(1)} %get-tuple-element.49) | copy-start | bytes 196612
  33.9 23.1 %copy-start.46 = (f32[256,2]{0,1:T(2,128)}, f32[256,2]{0,1:T(2,128)S(1)}, u32[]{:S(2)}) copy-start(f32[256,2]{0,1:T(2,128)S(1)} %copy.161) | copy-start | bytes 6148
  64.8 36.0 %reduce-scatter.33.cloned.1.call-start = ((), (), s32[]{:S(2)}) async-start(), calls=%async_computation.25 | async-start | bytes 2359296 | tf_op jit(solution)/shard_map/reduce_scatter | solution.py:91
  75.4 31.2 %reduce-scatter.27.cloned.1.call-start = ((), (), s32[]{:S(2)}) async-start(), calls=%async_computation.22 | async-start | bytes 2359296 | tf_op jit(solution)/shard_map/reduce_scatter | solution.py:217
  97.4 21.7 %reduce-scatter.29.cloned.1.call-start = ((), (), s32[]{:S(2)}) async-start(), calls=%async_computation.23 | async-start | bytes 2359296 | tf_op jit(solution)/shard_map/reduce_scatter | solution.py:218
  100.7 45.8 %reduce-scatter.35.cloned.1.call-start = ((), (), s32[]{:S(2)}) async-start(), calls=%async_computation.26 | async-start | bytes 786432 | tf_op jit(solution)/shard_map/reduce_scatter | solution.py:87
  130.5 32.7 %reduce-scatter.31.cloned.1.call-start = ((), (), s32[]{:S(2)}) async-start(), calls=%async_computation.24 | async-start | bytes 786432 | tf_op jit(solution)/shard_map/reduce_scatter | solution.py:87
  136.9 45.3 %reduce-scatter.37.cloned.1.call-start = ((), (), s32[]{:S(2)}) async-start(), calls=%async_computation.27 | async-start | bytes 1572864 | tf_op jit(solution)/shard_map/reduce_scatter | solution.py:91
  173.5 55.1 %reduce-scatter.39.cloned.1.call-start = ((), (), s32[]{:S(2)}) async-start(), calls=%async_computation.28 | async-start | bytes 786432 | tf_op jit(solution)/shard_map/reduce_scatter | solution.py:87
  210.9 88.3 %reduce-scatter.47.cloned.1.call-start = ((), (), s32[]{:S(2)}) async-start(), calls=%async_computation.32 | async-start | bytes 2359296 | tf_op jit(solution)/shard_map/reduce_scatter | solution.py:282
  212.7 153.4 %reduce-scatter.43.cloned.1.call-start = ((), (), s32[]{:S(2)}) async-start(), calls=%async_computation.30 | async-start | bytes 1179648 | tf_op jit(solution)/shard_map/reduce_scatter | solution.py:280
  214.2 218.3 %reduce-scatter.45.cloned.1.call-start = ((), (), s32[]{:S(2)}) async-start(), calls=%async_computation.31 | async-start | bytes 1179648 | tf_op jit(solution)/shard_map/reduce_scatter | solution.py:281
  216.6 293.8 %reduce-scatter.49.cloned.1.call-start = ((), (), s32[]{:S(2)}) async-start(), calls=%async_computation.33 | async-start | bytes 3538944 | tf_op jit(solution)/shard_map/reduce_scatter | solution.py:283
  219.0 369.3 %reduce-scatter.51.cloned.1.call-start = ((), (), s32[]{:S(2)}) async-start(), calls=%async_computation.34 | async-start | bytes 3538944 | tf_op jit(solution)/shard_map/reduce_scatter | solution.py:284
  222.4 443.8 %reduce-scatter.53.cloned.1.call-start = ((), (), s32[]{:S(2)}) async-start(), calls=%async_computation.35 | async-start | bytes 3538944 | tf_op jit(solution)/shard_map/reduce_scatter | solution.py:285
  225.9 511.6 %reduce-scatter.41.cloned.1.call-start = ((), (), s32[]{:S(2)}) async-start(), calls=%async_computation.29 | async-start | bytes 2359296 | tf_op jit(solution)/shard_map/reduce_scatter | solution.py:279
  227.8 47.3 %copy-start.40 = (f32[128,512]{1,0:T(8,128)S(1)}, f32[128,512]{1,0:T(8,128)}, u32[]{:S(2)}) copy-start(f32[128,512]{1,0:T(8,128)} %get-tuple-element.29) | copy-start | bytes 786436
  227.8 47.3 %copy-start.59 = (f32[128]{0:T(128)S(1)}, f32[128]{0:T(128)}, u32[]{:S(2)}) copy-start(f32[128]{0:T(128)} %get-tuple-element.50) | copy-start | bytes 1540
  (55 other events, 150.6 us)
Sparse Core Ops, SparseCore 0:
  22.9 9.4 reduce-scatter.20
  34.7 9.1 reduce-scatter.18
  46.1 9.6 reduce-scatter.22
  64.9 15.7 reduce-scatter.24
  82.7 9.0 reduce-scatter.32
  97.5 9.0 reduce-scatter.26
  108.8 10.2 reduce-scatter.28
  130.7 15.7 reduce-scatter.34
  148.7 14.5 reduce-scatter.30
  173.6 8.5 reduce-scatter.36
  211.0 15.6 reduce-scatter.38
  231.1 68.0 reduce-scatter.46
  303.6 62.4 reduce-scatter.42
  369.9 62.4 reduce-scatter.44
  436.9 73.5 reduce-scatter.48
  514.9 73.3 reduce-scatter.50
  592.7 73.4 reduce-scatter.52
  670.6 66.8 reduce-scatter.40
where the time goes:
time: 745 us; the launch traced here: 744 us
  waiting for transfers between devices  537 us (72%)
  blocking collectives  94.4 us (13%)
  matrix products  42.2 us (6%)
  other arithmetic  31.7 us (4%)
  local copies, waits for them, and re-layouts  23.1 us (3%)
  between operations  15.1 us (2%)
    reduce_scatter x1, waiting for transfers between devices, shards(): lax.psum_scatter(gate_part, 'dp', scatter_dimension=0, tiled=True)  78 us
    reduce_scatter x1, waiting for transfers between devices, shards(): lax.psum_scatter(down_part, 'dp', scatter_dimension=0, tiled=True)  77.9 us
    reduce_scatter x1, waiting for transfers between devices, shards(): lax.psum_scatter(up_weight_part, 'dp', scatter_dimension=0, tiled=True)  77.8 us
    reduce_scatter x1, waiting for transfers between devices, shards(): lax.psum_scatter(query_part, 'dp', scatter_dimension=0, tiled=True)  71.2 us
    reduce_scatter x1, waiting for transfers between devices, shards(): lax.psum_scatter(key_part, 'dp', scatter_dimension=0, tiled=True)  66.9 us
    reduce_scatter x1, waiting for transfers between devices, shards(): lax.psum_scatter(value_part, 'dp', scatter_dimension=0, tiled=True)  66.4 us
    psum x1, blocking collectives, shards(): lax.psum((attn_full, gain_query_part, gain_key_part, mlp_full), ('dp', 'r...  41.3 us
    all_gather x4, blocking collectives, gather_tokens(): return lax.all_gather(local, 'row', axis=0, tiled=True)  26.1 us
  transfers between devices with their start and end apart: 18, of which 16 were waited for; matrix products, arithmetic and copies ran while one was open for 6% of the time, Pallas kernels for 0%

commit v1 on v0

v1 whole, which is shorter than its diff:
```python
import math

import jax
import jax.numpy as jnp
from jax import lax
from jax.sharding import PartitionSpec as P

EPS = 1e-06
THETA = 1000000.0
NEGATIVE = -1e30


def layout(lengths, groups, group, slots):
    count = lengths.shape[0]
    mine = groups == group
    sizes_here = jnp.where(mine, lengths, 0)
    starts = jnp.cumsum(sizes_here) - sizes_here
    place = lax.broadcasted_iota(jnp.int32, (slots, count), 0)
    number = lax.broadcasted_iota(jnp.int32, (slots, count), 1)
    inside = mine[None, :] & (place >= starts[None, :]) & (place < (starts + sizes_here)[None, :])
    found = jnp.sum(inside.astype(jnp.int32), axis=1)
    segment = jnp.sum(jnp.where(inside, number, 0), axis=1)
    spot = lax.broadcasted_iota(jnp.int32, (slots,), 0)
    segment = jnp.where(found > 0, segment, count + spot)
    position = jnp.sum(jnp.where(inside, place - starts[None, :], 0), axis=1)
    return (segment, position)


def rotate(value_rows, position):
    size = value_rows.shape[-1]
    half = size // 2
    freq = THETA ** (-(jnp.arange(half, dtype=jnp.float32) * 2.0 / size))
    angle = position.astype(jnp.float32)[:, None] * freq[None, :]
    cosine = jnp.cos(angle)[:, None, :]
    sine = jnp.sin(angle)[:, None, :]
    first = value_rows[..., :half]
    second = value_rows[..., half:]
    return jnp.concatenate(
        [first * cosine - second * sine, second * cosine + first * sine], axis=-1
    )


def rms_scale(value_rows, gain):
    return (
        value_rows
        * lax.rsqrt(jnp.mean(value_rows * value_rows, axis=-1, keepdims=True) + EPS)
        * gain
    )


def swiglu(gate, up_part):
    return jax.nn.silu(gate) * up_part


def product(left, right):
    return jnp.dot(left, right, preferred_element_type=jnp.float32)


def contract_rows(left, right):
    return lax.dot_general(
        left, right, (((0,), (0,)), ((), ())), preferred_element_type=jnp.float32
    )


def contract_cols(left, right):
    return lax.dot_general(
        left, right, (((1,), (1,)), ((), ())), preferred_element_type=jnp.float32
    )


def attend(query_low, key_low, value_low, allowed, scale):
    token_rows, key_heads, head_dim = key_low.shape
    rank_share = query_low.shape[1] // key_heads
    grouped = query_low.reshape(token_rows, key_heads, rank_share, head_dim)
    raw = jnp.einsum("qhgd,khd->hgqk", grouped, key_low, preferred_element_type=jnp.float32)
    scores = jnp.where(allowed, raw * scale, NEGATIVE)
    top = jnp.max(scores, axis=-1, keepdims=True)
    exponent = jnp.exp(scores - top)
    total = jnp.sum(exponent, axis=-1, keepdims=True)
    probs = exponent / total
    attended = jnp.einsum(
        "hgqk,khd->qhgd", probs.astype(jnp.bfloat16), value_low, preferred_element_type=jnp.float32
    )
    return (attended.reshape(token_rows, key_heads * rank_share, head_dim), probs)


def attend_back(query_low, key_low, value_low, attended_grad, probs, scale):
    token_rows, key_heads, head_dim = key_low.shape
    rank_share = query_low.shape[1] // key_heads
    grouped = query_low.reshape(token_rows, key_heads, rank_share, head_dim)
    grad_grouped = attended_grad.reshape(token_rows, key_heads, rank_share, head_dim)
    prob_grad = jnp.einsum(
        "qhgd,khd->hgqk", grad_grouped, value_low, preferred_element_type=jnp.float32
    )
    inner = jnp.sum(probs * prob_grad, axis=-1, keepdims=True)
    score_grad = (probs * (prob_grad - inner)).astype(jnp.bfloat16)
    query_grad = (
        jnp.einsum("hgqk,khd->qhgd", score_grad, key_low, preferred_element_type=jnp.float32)
        * scale
    )
    key_grad = (
        jnp.einsum("hgqk,qhgd->khd", score_grad, grouped, preferred_element_type=jnp.float32)
        * scale
    )
    value_grad = jnp.einsum(
        "hgqk,qhgd->khd",
        probs.astype(jnp.bfloat16),
        grad_grouped,
        preferred_element_type=jnp.float32,
    )
    return (
        query_grad.reshape(token_rows, key_heads * rank_share, head_dim),
        key_grad,
        value_grad.astype(jnp.bfloat16),
    )


def swap(value, axis):
    return lax.ppermute(value, axis, [(0, 1), (1, 0)])


def flip(value, axis, bit):
    size = lax.axis_size(axis)
    return lax.ppermute(value, axis, [(i, i ^ bit) for i in range(size)])


def relative_order(size):
    bits = size.bit_length() - 1
    return [int(format(k, "b").zfill(bits)[::-1], 2) if bits else 0 for k in range(size)]


def relative_blocks(value_rows, axis):
    size = lax.axis_size(axis)
    me = lax.axis_index(axis)
    width = value_rows.shape[1] // size
    turned = value_rows.T.reshape(size, width, value_rows.shape[0])
    parts = [
        lax.dynamic_index_in_dim(turned, me ^ j, 0, keepdims=False) for j in relative_order(size)
    ]
    return jnp.concatenate(parts, axis=0)


def scattered_product(left, right, axis):
    size = lax.axis_size(axis)
    blocks = relative_blocks(left, axis)
    half = blocks.shape[0] // 2
    away = product(blocks[half:], right).astype(jnp.bfloat16)
    arrived = flip(away, axis, 1)
    kept = product(blocks[:half], right) + arrived.astype(jnp.float32)
    bit = 2
    while bit < size:
        half = kept.shape[0] // 2
        arrived = flip(kept[half:].astype(jnp.bfloat16), axis, bit)
        kept = kept[:half] + arrived.astype(jnp.float32)
        bit *= 2
    return kept


def total_over(value, axis):
    size = lax.axis_size(axis)
    bit = 1
    while bit < size:
        value = value + flip(value, axis, bit)
        bit *= 2
    return value


def pick(value, index, dim):
    half = value.shape[dim] // 2
    return lax.dynamic_slice_in_dim(value, index * half, half, dim)


def shards(
    tokens,
    cotangent,
    w_query,
    key_weight,
    value_weight,
    w_output,
    w_gate,
    w_up,
    w_down,
    gain_attn,
    gain_query,
    gain_key,
    gain_mlp,
    seq_lengths,
    seq_groups,
):
    half_rows, columns = tokens.shape
    width = columns * 2
    group_rows = half_rows * 2
    head_dim = gain_query.shape[0]
    scale = 1.0 / math.sqrt(head_dim)
    row = lax.axis_index("row")
    col = lax.axis_index("col")
    mine, theirs = col, 1 - col
    low = jnp.bfloat16

    def exchange_tokens(local):
        own = jnp.concatenate([local, swap(local, "row")], axis=0)
        return own, swap(own, "col")

    x_own_low, x_other_low = exchange_tokens(tokens)
    gains_own = jnp.stack([gain_attn, gain_mlp])
    gains_other = swap(gains_own, "col")
    qkv_keep = jnp.concatenate(
        [pick(w_query, mine, 1), pick(key_weight, mine, 1), pick(value_weight, mine, 1)], axis=1
    )
    qkv_other = swap(
        jnp.concatenate(
            [pick(w_query, theirs, 1), pick(key_weight, theirs, 1), pick(value_weight, theirs, 1)],
            axis=1,
        ),
        "col",
    )
    mlp_keep = jnp.concatenate([pick(w_gate, mine, 1), pick(w_up, mine, 1)], axis=1)
    mlp_theirs = jnp.concatenate([pick(w_gate, theirs, 1), pick(w_up, theirs, 1)], axis=1)
    mlp_other = swap(mlp_theirs, "col")
    output_mine, output_theirs = pick(w_output, mine, 0), pick(w_output, theirs, 0)
    output_other = swap(output_theirs, "col")
    down_mine, down_theirs = pick(w_down, mine, 0), pick(w_down, theirs, 0)
    down_other = swap(down_theirs, "col")
    cot_own, cot_other = exchange_tokens(cotangent)

    segment, position = layout(seq_lengths, seq_groups, lax.axis_index("dp"), group_rows)

    def own_first(vector):
        return jnp.where(row == 0, vector, jnp.roll(vector, half_rows))

    spot = own_first(lax.iota(jnp.int32, group_rows))
    segment, position = own_first(segment), own_first(position)
    allowed = (segment[:, None] == segment[None, :]) & (spot[None, :] <= spot[:, None])

    x_own = x_own_low.astype(jnp.float32)
    x_other = x_other_low.astype(jnp.float32)

    def inverse_of(own, other):
        total = jnp.sum(own * own, axis=1) + jnp.sum(other * other, axis=1)
        return lax.rsqrt(total / width + EPS)[:, None]

    inverse_attn = inverse_of(x_own, x_other)
    normed_own = (x_own * inverse_attn * gains_own[0]).astype(low)
    normed_other = (x_other * inverse_attn * gains_other[0]).astype(low)
    sums = product(normed_own, qkv_keep) + product(normed_other, qkv_other)
    query_wide = w_query.shape[1] // 2
    key_wide = key_weight.shape[1] // 2
    query_heads = query_wide // head_dim
    key_heads = key_wide // head_dim
    query_sum = sums[:, :query_wide]
    key_sum = sums[:, query_wide : query_wide + key_wide]
    value_sum = sums[:, query_wide + key_wide :]

    def turn(value_rows, gain):
        return rotate(rms_scale(value_rows, gain), position)

    query_rot, query_pull = jax.vjp(
        turn, query_sum.reshape(group_rows, query_heads, head_dim), gain_query
    )
    key_rot, key_pull = jax.vjp(turn, key_sum.reshape(group_rows, key_heads, head_dim), gain_key)
    query_low = query_rot.astype(low)
    key_low = key_rot.astype(low)
    value_low = value_sum.astype(low).reshape(group_rows, key_heads, head_dim)
    attended, probs = attend(query_low, key_low, value_low, allowed, scale)
    attended_own = attended.reshape(group_rows, query_wide).astype(low)
    attended_other = swap(attended_own, "col")
    partial_out = product(attended_own, output_mine) + product(attended_other, output_theirs)
    hidden = x_own + partial_out + swap(partial_out.astype(low), "row").astype(
        jnp.float32
    )[jnp.r_[half_rows:group_rows, 0:half_rows]]
    hidden_low_other = swap(hidden.astype(low), "col")
    hidden_other = hidden_low_other.astype(jnp.float32)
    inverse_mlp = inverse_of(hidden, hidden_other)
    mlp_own = (hidden * inverse_mlp * gains_own[1]).astype(low)
    mlp_rest = (hidden_other * inverse_mlp * gains_other[1]).astype(low)
    both = product(mlp_own, mlp_keep) + product(mlp_rest, mlp_other)
    units = both.shape[1] // 2
    gate, up_part = both[:, :units], both[:, units:]
    activated, swish_pull = jax.vjp(swiglu, gate, up_part)
    act_grad = contract_cols(cot_own, down_mine) + contract_cols(cot_other, down_other)
    gate_grad, up_grad = swish_pull(act_grad)
    grads_own = jnp.concatenate([gate_grad, up_grad], axis=1).astype(low)
    grads_other = swap(grads_own, "col")
    mlp_partial = contract_cols(grads_own, mlp_keep) + contract_cols(grads_other, mlp_theirs)
    normed_mlp_grad = mlp_partial + swap(mlp_partial.astype(low), "row").astype(
        jnp.float32
    )[jnp.r_[half_rows:group_rows, 0:half_rows]]
    grad_other = swap(normed_mlp_grad.astype(low), "col").astype(jnp.float32)
    scaled_own = normed_mlp_grad * gains_own[1]
    scaled_other = grad_other * gains_other[1]
    inner = (
        jnp.sum(scaled_own * hidden, axis=1) + jnp.sum(scaled_other * hidden_other, axis=1)
    )[:, None] / width
    cube = inverse_mlp**3 * inner
    hidden_grad = cot_own.astype(jnp.float32) + inverse_mlp * scaled_own - hidden * cube
    hidden_grad_other = (
        cot_other.astype(jnp.float32) + inverse_mlp * scaled_other - hidden_other * cube
    )
    gain_mlp_part = jnp.sum(
        (normed_mlp_grad * hidden * inverse_mlp)[:half_rows], axis=0
    )
    back_own = hidden_grad.astype(low)
    back_other = hidden_grad_other.astype(low)
    attended_grad = (
        contract_cols(back_own, output_mine) + contract_cols(back_other, output_other)
    ).astype(low)
    query_grad, key_grad, value_grad = attend_back(
        query_low,
        key_low,
        value_low,
        attended_grad.reshape(group_rows, query_heads, head_dim),
        probs,
        scale,
    )
    query_pre, gain_query_part = query_pull(query_grad)
    key_pre, gain_key_part = key_pull(key_grad)
    pre_own = jnp.concatenate(
        [
            query_pre.reshape(group_rows, query_wide).astype(low),
            key_pre.reshape(group_rows, key_wide).astype(low),
            value_grad.reshape(group_rows, key_wide),
        ],
        axis=1,
    )
    pre_other = swap(pre_own, "col")

    def whole(own, other, dim):
        first = jnp.where(col == 0, own, other)
        second = jnp.where(col == 0, other, own)
        return jnp.concatenate([first, second], axis=dim)

    qkv_theirs = jnp.concatenate(
        [pick(w_query, theirs, 1), pick(key_weight, theirs, 1), pick(value_weight, theirs, 1)],
        axis=1,
    )
    attn_partial = contract_cols(pre_own, qkv_keep) + contract_cols(pre_other, qkv_theirs)
    arrived = swap(attn_partial[half_rows:].astype(low), "row")
    normed_attn_grad = attn_partial[:half_rows] + arrived.astype(jnp.float32)
    x_mine = x_own[:half_rows]
    inverse_mine = inverse_attn[:half_rows]
    scaled = normed_attn_grad * gain_attn
    dot = jnp.sum(scaled * x_mine, axis=1).reshape(1, half_rows)
    dot = ((dot + swap(dot, "col")) / width).reshape(half_rows, 1)
    input_grad = (
        hidden_grad[:half_rows] + inverse_mine * scaled - x_mine * inverse_mine**3 * dot
    )
    gain_attn_part = jnp.sum(normed_attn_grad * x_mine * inverse_mine, axis=0)

    activated_own = activated.astype(low)
    activated_other = swap(activated_own, "col")
    down_partial = product(activated_own, down_mine) + product(activated_other, down_theirs)
    mixed = (
        hidden[:half_rows]
        + down_partial[:half_rows]
        + swap(down_partial[half_rows:].astype(low), "row").astype(jnp.float32)
    ).astype(low)

    down_total = scattered_product(whole(activated_own, activated_other, 1), cot_own, "dp")
    grads_first = jnp.where(col == 0, grads_own, grads_other)
    grads_second = jnp.where(col == 0, grads_other, grads_own)
    mlp_total = scattered_product(
        mlp_own,
        jnp.concatenate(
            [
                grads_first[:, :units],
                grads_second[:, :units],
                grads_first[:, units:],
                grads_second[:, units:],
            ],
            axis=1,
        ),
        "dp",
    )
    output_total = scattered_product(whole(attended_own, attended_other, 1), back_own, "dp")
    pre_first = jnp.where(col == 0, pre_own, pre_other)
    pre_second = jnp.where(col == 0, pre_other, pre_own)
    cuts = (0, query_wide, query_wide + key_wide, query_wide + 2 * key_wide)
    pre_whole = jnp.concatenate(
        [
            part[:, cuts[i] : cuts[i + 1]]
            for i in range(3)
            for part in (pre_first, pre_second)
        ],
        axis=1,
    )
    qkv_total = scattered_product(normed_own, pre_whole, "dp")
    edge = 2 * query_wide
    step = 2 * key_wide

    small = jnp.concatenate([gain_attn_part, gain_mlp_part, gain_query_part, gain_key_part])
    small = small.reshape(-1, 128)
    small = total_over(total_over(small, "dp"), "row").reshape(-1)
    heads_part = small[2 * columns :]
    heads_part = heads_part + swap(heads_part, "col")
    return (
        mixed,
        input_grad,
        qkv_total[:, :edge],
        qkv_total[:, edge : edge + step],
        qkv_total[:, edge + step :],
        output_total,
        mlp_total[:, : 2 * units],
        mlp_total[:, 2 * units :],
        down_total,
        small[:columns],
        heads_part[:head_dim],
        heads_part[head_dim:],
        small[columns : 2 * columns],
    )


def solution(mesh):
    in_specs = (
        P(("dp", "row"), "col"),
        P(("dp", "row"), "col"),
        P("col", "row"),
        P("col", "row"),
        P("col", "row"),
        P("row", "col"),
        P("col", "row"),
        P("col", "row"),
        P("row", "col"),
        P("col"),
        P(),
        P(),
        P("col"),
        P(),
        P(),
    )
    out_specs = (
        P(("dp", "row"), "col"),
        P(("dp", "row"), "col"),
        P(("col", "dp"), "row"),
        P(("col", "dp"), "row"),
        P(("col", "dp"), "row"),
        P(("row", "dp"), "col"),
        P(("col", "dp"), "row"),
        P(("col", "dp"), "row"),
        P(("row", "dp"), "col"),
        P("col"),
        P(),
        P(),
        P("col"),
    )
    return jax.shard_map(shards, mesh=mesh, in_specs=in_specs, out_specs=out_specs, check_vma=False)
```

time: 745 us -> 262 us (0.35)
  waiting for transfers between devices: 537 us -> 108 us
  blocking collectives: 94.4 us -> 0 us
  starting transfers between devices: 0.93 us -> 32.6 us
  local copies, waits for them, and re-layouts: 23.1 us -> 40.9 us
  between operations: 15.1 us -> 2.39 us
    reduce_scatter x18 -> x0, waiting for transfers between devices: 537 us -> none  [the longest x1 78 us: shards(): lax.psum_scatter(gate_part, 'dp', scatter_dimension=0, tiled=True)]
    ppermute x0 -> x37, waiting for transfers between devices: none -> 108 us  [the longest x16 94 us: flip(): return lax.ppermute(value, axis, [(i, i ^ bit) for i in range(size)])]
    psum x5 -> x0, blocking collectives: 52.4 us -> none  [the longest x1 41.3 us: shards(): lax.psum((attn_full, gain_query_part, gain_key_part, mlp_full), ('dp', 'r...]
    all_gather x11 -> x0, blocking collectives: 42 us -> none  [the longest x4 26.1 us: gather_tokens(): return lax.all_gather(local, 'row', axis=0, tiled=True)]
    ppermute x0 -> x37, starting transfers between devices: none -> 32.6 us  [the longest x16 22.1 us: flip(): return lax.ppermute(value, axis, [(i, i ^ bit) for i in range(size)])]
    dot_general x8 -> x0, matrix products: 14.6 us -> none  [the longest x7 14.2 us: contract_rows(): lax.dot_general(left, right, (((0,), (0,)), ((), ())), preferred_element_...]
    slice x0 -> x28, local copies, waits for them, and re-layouts: none -> 9.47 us  [the longest x8 1.11 us: scattered_product(): arrived = flip(kept[half:].astype(jnp.bfloat16), axis, bit)]
    unnamed x125 -> x206, local copies, waits for them, and re-layouts: 14.1 us -> 4.66 us
  transfers between devices with their start and end apart: 18 -> 37, of which waited for: 16 -> 14; matrix products, arithmetic and copies ran while one was open for 6% -> 44% of each run, Pallas kernels for 0% -> 0%
where the time goes in v1:
time: 262 us; the launch traced here: 261 us
  waiting for transfers between devices  108 us (41%)
  local copies, waits for them, and re-layouts  40.9 us (16%)
  matrix products  39.2 us (15%)
  other arithmetic  38 us (15%)
  starting transfers between devices  32.6 us (12%)
    ppermute x16, waiting for transfers between devices, flip(): return lax.ppermute(value, axis, [(i, i ^ bit) for i in range(size)])  94 us
    ppermute x16, starting transfers between devices, flip(): return lax.ppermute(value, axis, [(i, i ^ bit) for i in range(size)])  22.1 us
    dot_general x16, matrix products, product(): return jnp.dot(left, right, preferred_element_type=jnp.float32)  17.1 us
    ppermute x21, waiting for transfers between devices, swap(): return lax.ppermute(value, axis, [(0, 1), (1, 0)])  13.8 us
    dot_general x8, matrix products, contract_cols(): lax.dot_general(left, right, (((1,), (1,)), ((), ())), preferred_element_...  12 us
    ppermute x21, starting transfers between devices, swap(): return lax.ppermute(value, axis, [(0, 1), (1, 0)])  10.5 us
    dynamic_slice x5, local copies, waits for them, and re-layouts, pick(): return lax.dynamic_slice_in_dim(value, index * half, half, dim)  7.57 us
  transfers between devices with their start and end apart: 37, of which 14 were waited for; matrix products, arithmetic and copies ran while one was open for 44% of the time, Pallas kernels for 0%

profile of v1, /device:TPU:0, one launch (start us, length us, event | category | flops | bytes accessed | tf_op | source)
XLA Modules:
  0.0 260.7 jit_solution(14564023338043838337)
XLA Ops:
  0.7 3.0 %collective-permute-start = (bf16[128,512]{1,0:T(8,128)(2,1)}, bf16[128,512]{1,0:T(8,128)(2,1)}, u32[]{:S(2)}, u32[]{:S(2)}) collective-permute-start(bf16[128,512]{1,0:T(8,128)(2,1)} %param.15), channel_id=1, source_target_pairs={{0,2},{2,0},{1,3},{3,1},{4,6},{6,4},{5,7},{7,5},{8,10},{10,8},{9,1... | collective-permute-start | bytes 393224 | tf_op jit(solution)/shard_map/ppermute | solution.py:119
  9.0 2.8 %constant_dynamic-slice_fusion.1 = (bf16[512,768]{1,0:T(8,128)(2,1)S(1)}, bf16[512,768]{1,0:T(8,128)(2,1)}, bf16[512,768]{1,0:T(8,128)(2,1)}, bf16[512,768]{1,0:T(8,128)(2,1)S(1)}) fusion(bf16[512,1536]{1,0:T(8,128)(2,1)S(1)} %copy-done.26, s32[]{:T(128)S(6)} %select_n.217, s32[]{:T(128)S(6)} %select_n.216, bf16[512,1536]{1,0:T(8,128)(2,1)} %param.21), kind=kLoop, calls=%fused_computation.277 | loop fusion | bytes 6291464 | tf_op jit(solution)/shard_map/dynamic_slice | solution.py:170
  43.8 3.3 %fusion.161 = (f32[2,2,256]{2,1,0:T(2,128)}, f32[2,2,256,256]{2,3,1,0:T(8,128)}) fusion(pred[256,256]{0,1:T(8,128)(4,1)} %compare_and_fusion, bf16[256,2,64]{2,0,1:T(8,128)(2,1)} %get-tuple-element.84, bf16[256,2,64]{2,0,1:T(8,128)(2,1)} %get-tuple-element.83, bf16[256,2,2,64]{3,0,2,1:T(8,128)(2,1)} %bitcast.224, bf16[256,2,2,64]{3,0,2,1:T(8,128)(2,1)} %bitcast.220), kind=kOutput, calls=%fused_computation.354 | convolution fusion | flops 68944128 | bytes 1511424 | tf_op jit(solution)/shard_map/sub | solution.py:78
  51.2 2.5 fusion.164
  54.0 2.1 fusion.162
  58.8 5.8 %collective-permute-done.5 = bf16[256,512]{1,0:T(8,128)(2,1)S(1)} collective-permute-done((bf16[256,512]{1,0:T(8,128)(2,1)S(1)}, bf16[256,512]{1,0:T(8,128)(2,1)S(1)}, u32[]{:S(2)}, u32[]{:S(2)}) %collective-permute-start.5) | collective-permute-done | bytes 262176 | tf_op jit(solution)/shard_map/ppermute | solution.py:119
  66.8 2.1 fusion.150
  86.6 2.2 convolution_convert_fusion.2
  90.4 2.5 fusion.163
  96.7 4.4 %collective-permute-done.14 = bf16[256,512]{1,0:T(8,128)(2,1)S(1)} collective-permute-done((bf16[256,512]{1,0:T(8,128)(2,1)S(1)}, bf16[256,512]{1,0:T(8,128)(2,1)S(1)}, u32[]{:S(2)}, u32[]{:S(2)}) %collective-permute-start.14) | collective-permute-done | bytes 262176 | tf_op jit(solution)/shard_map/ppermute | solution.py:119
  103.8 2.2 fusion.54
  106.0 2.9 %collective-permute-done.29 = bf16[768,512]{1,0:T(8,128)(2,1)} collective-permute-done((bf16[768,512]{1,0:T(8,128)(2,1)}, bf16[768,512]{1,0:T(8,128)(2,1)}, u32[]{:S(2)}, u32[]{:S(2)}) %collective-permute-start.29) | collective-permute-done | bytes 786464 | tf_op jit(solution)/shard_map/ppermute | solution.py:124
  120.4 2.4 fusion.8
  133.6 2.7 %collective-permute-start.31 = (bf16[192,512]{1,0:T(8,128)(2,1)S(1)}, bf16[192,512]{1,0:T(8,128)(2,1)S(1)}, u32[]{:S(2)}, u32[]{:S(2)}) collective-permute-start(bf16[192,512]{1,0:T(8,128)(2,1)S(1)} %slice.429), channel_id=1, source_target_pairs={{0,16},{4,20},{8,24},{12,28},{16,0},{20,4},{24,8},{28,12},{1,17},{... | collective-permute-start | bytes 589832 | tf_op jit(solution)/shard_map/ppermute | solution.py:124
  138.6 7.2 %collective-permute-done.31 = bf16[192,512]{1,0:T(8,128)(2,1)S(1)} collective-permute-done((bf16[192,512]{1,0:T(8,128)(2,1)S(1)}, bf16[192,512]{1,0:T(8,128)(2,1)S(1)}, u32[]{:S(2)}, u32[]{:S(2)}) %collective-permute-start.31) | collective-permute-done | bytes 196640 | tf_op jit(solution)/shard_map/ppermute | solution.py:124
  150.8 2.9 %collective-permute-done.18 = bf16[128,512]{1,0:T(8,128)(2,1)S(1)} collective-permute-done((bf16[128,512]{1,0:T(8,128)(2,1)S(1)}, bf16[128,512]{1,0:T(8,128)(2,1)S(1)}, u32[]{:S(2)}, u32[]{:S(2)}) %collective-permute-start.18) | collective-permute-done | bytes 131104 | tf_op jit(solution)/shard_map/ppermute | solution.py:119
  154.6 24.6 %collective-permute-done.32 = f32[10,128]{1,0:T(8,128)S(1)} collective-permute-done((f32[10,128]{1,0:T(8,128)S(1)}, f32[10,128]{1,0:T(8,128)S(1)}, u32[]{:S(2)}, u32[]{:S(2)}) %collective-permute-start.32) | collective-permute-done | bytes 5152 | tf_op jit(solution)/shard_map/ppermute | solution.py:124
  183.5 2.7 %collective-permute-start.34 = (f32[10,128]{1,0:T(8,128)S(1)}, f32[10,128]{1,0:T(8,128)S(1)}, u32[]{:S(2)}, u32[]{:S(2)}) collective-permute-start(f32[10,128]{1,0:T(8,128)S(1)} %fusion.187), channel_id=1, source_target_pairs={{0,16},{4,20},{8,24},{12,28},{16,0},{20,4},{24,8},{28,12},{1,17},{... | collective-permute-start | bytes 15368 | tf_op jit(solution)/shard_map/ppermute | solution.py:124
  189.5 2.3 collective-permute-done.35
  193.0 2.7 %collective-permute-start.25 = (bf16[128,512]{1,0:T(8,128)(2,1)S(1)}, bf16[128,512]{1,0:T(8,128)(2,1)S(1)}, u32[]{:S(2)}, u32[]{:S(2)}) collective-permute-start(bf16[128,512]{1,0:T(8,128)(2,1)S(1)} %slice.430), channel_id=1, source_target_pairs={{0,16},{4,20},{8,24},{12,28},{16,0},{20,4},{24,8},{28,12},{1,17},{... | collective-permute-start | bytes 393224 | tf_op jit(solution)/shard_map/ppermute | solution.py:124
  195.7 9.7 %collective-permute-done.20 = bf16[256,2048]{1,0:T(8,128)(2,1)S(1)} collective-permute-done((bf16[256,2048]{1,0:T(8,128)(2,1)S(1)}, bf16[256,2048]{1,0:T(8,128)(2,1)S(1)}, u32[]{:S(2)}, u32[]{:S(2)}) %collective-permute-start.20) | collective-permute-done | bytes 1048608 | tf_op jit(solution)/shard_map/ppermute | solution.py:124
  210.0 13.6 %collective-permute-done.21 = bf16[128,2048]{1,0:T(8,128)(2,1)S(1)} collective-permute-done((bf16[128,2048]{1,0:T(8,128)(2,1)S(1)}, bf16[128,2048]{1,0:T(8,128)(2,1)S(1)}, u32[]{:S(2)}, u32[]{:S(2)}) %collective-permute-start.21) | collective-permute-done | bytes 524320 | tf_op jit(solution)/shard_map/ppermute | solution.py:124
  225.6 15.2 %collective-permute-done.27 = bf16[128,3072]{1,0:T(8,128)(2,1)S(1)} collective-permute-done((bf16[128,3072]{1,0:T(8,128)(2,1)S(1)}, bf16[128,3072]{1,0:T(8,128)(2,1)S(1)}, u32[]{:S(2)}, u32[]{:S(2)}) %collective-permute-start.27) | collective-permute-done | bytes 786464 | tf_op jit(solution)/shard_map/ppermute | solution.py:124
  244.3 15.4 %collective-permute-done.28 = bf16[64,3072]{1,0:T(8,128)(2,1)S(1)} collective-permute-done((bf16[64,3072]{1,0:T(8,128)(2,1)S(1)}, bf16[64,3072]{1,0:T(8,128)(2,1)S(1)}, u32[]{:S(2)}, u32[]{:S(2)}) %collective-permute-start.28) | collective-permute-done | bytes 393248 | tf_op jit(solution)/shard_map/ppermute | solution.py:124
  (426 shorter events, 121.0 us)
Async XLA Ops:
  0.7 18.6 %collective-permute-start = (bf16[128,512]{1,0:T(8,128)(2,1)}, bf16[128,512]{1,0:T(8,128)(2,1)}, u32[]{:S(2)}, u32[]{:S(2)}) collective-permute-start(bf16[128,512]{1,0:T(8,128)(2,1)} %param.15), channel_id=1, source_target_pairs={{0,2},{2,0},{1,3},{3,1},{4,6},{6,4},{5,7},{7,5},{8,10},{10,8},{9,1... | collective-permute-start | bytes 393224 | tf_op jit(solution)/shard_map/ppermute | solution.py:119
  7.9 17.3 %collective-permute-start.3 = (bf16[512,1024]{1,0:T(8,128)(2,1)}, bf16[512,1024]{1,0:T(8,128)(2,1)}, u32[]{:S(2)}, u32[]{:S(2)}) collective-permute-start(bf16[512,1024]{1,0:T(8,128)(2,1)} %pad_maximum_fusion.4), channel_id=1, source_target_pairs={{0,1},{1,0},{2,3},{3,2},{4,5},{5,4},{6,7},{7,6},{8,9},{9,8},{10,11... | collective-permute-start | bytes 3145736 | tf_op jit(solution)/shard_map/ppermute | solution.py:119
  8.5 12.0 %collective-permute-start.2 = (f32[2,512]{1,0:T(2,128)}, f32[2,512]{1,0:T(2,128)S(1)}, u32[]{:S(2)}, u32[]{:S(2)}) collective-permute-start(f32[2,512]{1,0:T(2,128)} %pad_maximum_fusion.15), channel_id=1, source_target_pairs={{0,1},{1,0},{2,3},{3,2},{4,5},{5,4},{6,7},{7,6},{8,9},{9,8},{10,11... | collective-permute-start | bytes 12296 | tf_op jit(solution)/shard_map/ppermute | solution.py:119
  13.5 60.3 %collective-permute-start.7 = (bf16[512,1536]{1,0:T(8,128)(2,1)}, bf16[512,1536]{1,0:T(8,128)(2,1)}, u32[]{:S(2)}, u32[]{:S(2)}) collective-permute-start(bf16[512,1536]{1,0:T(8,128)(2,1)} %pad_maximum_fusion.1), channel_id=1, source_target_pairs={{0,1},{1,0},{2,3},{3,2},{4,5},{5,4},{6,7},{7,6},{8,9},{9,8},{10,11... | collective-permute-start | bytes 4718600 | tf_op jit(solution)/shard_map/ppermute | solution.py:119
  19.3 31.9 %collective-permute-start.12 = (bf16[768,512]{1,0:T(8,128)(2,1)}, bf16[768,512]{1,0:T(8,128)(2,1)}, u32[]{:S(2)}, u32[]{:S(2)}) collective-permute-start(bf16[768,512]{1,0:T(8,128)(2,1)} %constant_dynamic-slice_fusion), channel_id=1, source_target_pairs={{0,1},{1,0},{2,3},{3,2},{4,5},{5,4},{6,7},{7,6},{8,9},{9,8},{10,11... | collective-permute-start | bytes 2359304 | tf_op jit(solution)/shard_map/ppermute | solution.py:119
  21.7 93.6 %collective-permute-start.16 = (bf16[512,512]{1,0:T(8,128)(2,1)}, bf16[512,512]{1,0:T(8,128)(2,1)}, u32[]{:S(2)}, u32[]{:S(2)}) collective-permute-start(bf16[512,512]{1,0:T(8,128)(2,1)} %constant_dynamic-slice_fusion.5), channel_id=1, source_target_pairs={{0,1},{1,0},{2,3},{3,2},{4,5},{5,4},{6,7},{7,6},{8,9},{9,8},{10,11... | collective-permute-start | bytes 1572872 | tf_op jit(solution)/shard_map/ppermute | solution.py:119
  23.7 27.4 %collective-permute-start.11 = (bf16[256,512]{1,0:T(8,128)(2,1)}, bf16[256,512]{1,0:T(8,128)(2,1)}, u32[]{:S(2)}, u32[]{:S(2)}) collective-permute-start(bf16[256,512]{1,0:T(8,128)(2,1)} %constant_dynamic-update-slice_fusion.2), channel_id=1, source_target_pairs={{0,1},{1,0},{2,3},{3,2},{4,5},{5,4},{6,7},{7,6},{8,9},{9,8},{10,11... | collective-permute-start | bytes 786440 | tf_op jit(solution)/shard_map/ppermute | solution.py:119
  79.2 11.2 %collective-permute-start.13 = (bf16[256,1536]{1,0:T(8,128)(2,1)}, bf16[256,1536]{1,0:T(8,128)(2,1)}, u32[]{:S(2)}, u32[]{:S(2)}) collective-permute-start(bf16[256,1536]{1,0:T(8,128)(2,1)} %pad_maximum_fusion.7), channel_id=1, source_target_pairs={{0,1},{1,0},{2,3},{3,2},{4,5},{5,4},{6,7},{7,6},{8,9},{9,8},{10,11... | collective-permute-start | bytes 2359304 | tf_op jit(solution)/shard_map/ppermute | solution.py:119
  83.6 20.2 %collective-permute-start.9 = (bf16[128,512]{1,0:T(8,128)(2,1)}, bf16[128,512]{1,0:T(8,128)(2,1)}, u32[]{:S(2)}, u32[]{:S(2)}) collective-permute-start(bf16[128,512]{1,0:T(8,128)(2,1)} %slice.432), channel_id=1, source_target_pairs={{0,2},{2,0},{1,3},{3,1},{4,6},{6,4},{5,7},{7,5},{8,10},{10,8},{9,1... | collective-permute-start | bytes 393224 | tf_op jit(solution)/shard_map/ppermute | solution.py:119
  88.9 20.0 %collective-permute-start.29 = (bf16[768,512]{1,0:T(8,128)(2,1)}, bf16[768,512]{1,0:T(8,128)(2,1)}, u32[]{:S(2)}, u32[]{:S(2)}) collective-permute-start(bf16[768,512]{1,0:T(8,128)(2,1)} %convolution_convert_fusion.2), channel_id=1, source_target_pairs={{0,4},{4,0},{8,12},{12,8},{16,20},{20,16},{24,28},{28,24},{1,5},{5... | collective-permute-start | bytes 2359304 | tf_op jit(solution)/shard_map/ppermute | solution.py:124
  103.5 9.4 %collective-permute-start.15 = (bf16[256,512]{1,0:T(8,128)(2,1)S(1)}, bf16[256,512]{1,0:T(8,128)(2,1)S(1)}, u32[]{:S(2)}, u32[]{:S(2)}) collective-permute-start(bf16[256,512]{1,0:T(8,128)(2,1)S(1)} %get-tuple-element.22), channel_id=1, source_target_pairs={{0,1},{1,0},{2,3},{3,2},{4,5},{5,4},{6,7},{7,6},{8,9},{9,8},{10,11... | collective-permute-start | bytes 786440 | tf_op jit(solution)/shard_map/ppermute | solution.py:119
  111.3 21.2 %collective-permute-start.30 = (bf16[384,512]{1,0:T(8,128)(2,1)}, bf16[384,512]{1,0:T(8,128)(2,1)}, u32[]{:S(2)}, u32[]{:S(2)}) collective-permute-start(bf16[384,512]{1,0:T(8,128)(2,1)} %slice.425), channel_id=1, source_target_pairs={{0,8},{4,12},{8,0},{12,4},{16,24},{20,28},{24,16},{28,20},{1,9},{5... | collective-permute-start | bytes 1179656 | tf_op jit(solution)/shard_map/ppermute | solution.py:124
  130.4 16.2 %collective-permute-start.17 = (bf16[256,1024]{1,0:T(8,128)(2,1)}, bf16[256,1024]{1,0:T(8,128)(2,1)}, u32[]{:S(2)}, u32[]{:S(2)}) collective-permute-start(bf16[256,1024]{1,0:T(8,128)(2,1)} %pad_maximum_fusion.8), channel_id=1, source_target_pairs={{0,1},{1,0},{2,3},{3,2},{4,5},{5,4},{6,7},{7,6},{8,9},{9,8},{10,11... | collective-permute-start | bytes 1572872 | tf_op jit(solution)/shard_map/ppermute | solution.py:119
  130.9 17.9 %collective-permute-start.23 = (bf16[512,512]{1,0:T(8,128)(2,1)S(1)}, bf16[512,512]{1,0:T(8,128)(2,1)S(1)}, u32[]{:S(2)}, u32[]{:S(2)}) collective-permute-start(bf16[512,512]{1,0:T(8,128)(2,1)S(1)} %convolution_convert_fusion.3), channel_id=1, source_target_pairs={{0,4},{4,0},{8,12},{12,8},{16,20},{20,16},{24,28},{28,24},{1,5},{5... | collective-permute-start | bytes 1572872 | tf_op jit(solution)/shard_map/ppermute | solution.py:124
  133.6 12.1 %collective-permute-start.31 = (bf16[192,512]{1,0:T(8,128)(2,1)S(1)}, bf16[192,512]{1,0:T(8,128)(2,1)S(1)}, u32[]{:S(2)}, u32[]{:S(2)}) collective-permute-start(bf16[192,512]{1,0:T(8,128)(2,1)S(1)} %slice.429), channel_id=1, source_target_pairs={{0,16},{4,20},{8,24},{12,28},{16,0},{20,4},{24,8},{28,12},{1,17},{... | collective-permute-start | bytes 589832 | tf_op jit(solution)/shard_map/ppermute | solution.py:124
  138.0 69.6 %collective-permute-start.26 = (bf16[256,3072]{1,0:T(8,128)(2,1)S(1)}, bf16[256,3072]{1,0:T(8,128)(2,1)S(1)}, u32[]{:S(2)}, u32[]{:S(2)}) collective-permute-start(bf16[256,3072]{1,0:T(8,128)(2,1)S(1)} %convolution_convert_fusion), channel_id=1, source_target_pairs={{0,4},{4,0},{8,12},{12,8},{16,20},{20,16},{24,28},{28,24},{1,5},{5... | collective-permute-start | bytes 4718600 | tf_op jit(solution)/shard_map/ppermute | solution.py:124
  149.2 43.8 %collective-permute-start.24 = (bf16[256,512]{1,0:T(8,128)(2,1)S(1)}, bf16[256,512]{1,0:T(8,128)(2,1)S(1)}, u32[]{:S(2)}, u32[]{:S(2)}) collective-permute-start(bf16[256,512]{1,0:T(8,128)(2,1)S(1)} %slice.427), channel_id=1, source_target_pairs={{0,8},{4,12},{8,0},{12,4},{16,24},{20,28},{24,16},{28,20},{1,9},{5... | collective-permute-start | bytes 786440 | tf_op jit(solution)/shard_map/ppermute | solution.py:124
  153.9 25.3 %collective-permute-start.32 = (f32[10,128]{1,0:T(8,128)S(1)}, f32[10,128]{1,0:T(8,128)S(1)}, u32[]{:S(2)}, u32[]{:S(2)}) collective-permute-start(f32[10,128]{1,0:T(8,128)S(1)} %maximum_bitcast_fusion.2), channel_id=1, source_target_pairs={{0,4},{4,0},{8,12},{12,8},{16,20},{20,16},{24,28},{28,24},{1,5},{5... | collective-permute-start | bytes 15368 | tf_op jit(solution)/shard_map/ppermute | solution.py:124
  180.8 24.6 %collective-permute-start.20 = (bf16[256,2048]{1,0:T(8,128)(2,1)S(1)}, bf16[256,2048]{1,0:T(8,128)(2,1)S(1)}, u32[]{:S(2)}, u32[]{:S(2)}) collective-permute-start(bf16[256,2048]{1,0:T(8,128)(2,1)S(1)} %convolution_convert_fusion.1), channel_id=1, source_target_pairs={{0,4},{4,0},{8,12},{12,8},{16,20},{20,16},{24,28},{28,24},{1,5},{5... | collective-permute-start | bytes 3145736 | tf_op jit(solution)/shard_map/ppermute | solution.py:124
  193.0 16.3 %collective-permute-start.25 = (bf16[128,512]{1,0:T(8,128)(2,1)S(1)}, bf16[128,512]{1,0:T(8,128)(2,1)S(1)}, u32[]{:S(2)}, u32[]{:S(2)}) collective-permute-start(bf16[128,512]{1,0:T(8,128)(2,1)S(1)} %slice.430), channel_id=1, source_target_pairs={{0,16},{4,20},{8,24},{12,28},{16,0},{20,4},{24,8},{28,12},{1,17},{... | collective-permute-start | bytes 393224 | tf_op jit(solution)/shard_map/ppermute | solution.py:124
  205.9 17.7 %collective-permute-start.21 = (bf16[128,2048]{1,0:T(8,128)(2,1)S(1)}, bf16[128,2048]{1,0:T(8,128)(2,1)S(1)}, u32[]{:S(2)}, u32[]{:S(2)}) collective-permute-start(bf16[128,2048]{1,0:T(8,128)(2,1)S(1)} %slice.424), channel_id=1, source_target_pairs={{0,8},{4,12},{8,0},{12,4},{16,24},{20,28},{24,16},{28,20},{1,9},{5... | collective-permute-start | bytes 1572872 | tf_op jit(solution)/shard_map/ppermute | solution.py:124
  208.3 32.5 %collective-permute-start.27 = (bf16[128,3072]{1,0:T(8,128)(2,1)S(1)}, bf16[128,3072]{1,0:T(8,128)(2,1)S(1)}, u32[]{:S(2)}, u32[]{:S(2)}) collective-permute-start(bf16[128,3072]{1,0:T(8,128)(2,1)S(1)} %slice.423), channel_id=1, source_target_pairs={{0,8},{4,12},{8,0},{12,4},{16,24},{20,28},{24,16},{28,20},{1,9},{5... | collective-permute-start | bytes 2359304 | tf_op jit(solution)/shard_map/ppermute | solution.py:124
  223.8 19.0 %collective-permute-start.22 = (bf16[64,2048]{1,0:T(8,128)(2,1)S(1)}, bf16[64,2048]{1,0:T(8,128)(2,1)S(1)}, u32[]{:S(2)}, u32[]{:S(2)}) collective-permute-start(bf16[64,2048]{1,0:T(8,128)(2,1)S(1)} %slice.428), channel_id=1, source_target_pairs={{0,16},{4,20},{8,24},{12,28},{16,0},{20,4},{24,8},{28,12},{1,17},{... | collective-permute-start | bytes 786440 | tf_op jit(solution)/shard_map/ppermute | solution.py:124
  241.1 18.6 %collective-permute-start.28 = (bf16[64,3072]{1,0:T(8,128)(2,1)S(1)}, bf16[64,3072]{1,0:T(8,128)(2,1)S(1)}, u32[]{:S(2)}, u32[]{:S(2)}) collective-permute-start(bf16[64,3072]{1,0:T(8,128)(2,1)S(1)} %slice.426), channel_id=1, source_target_pairs={{0,16},{4,20},{8,24},{12,28},{16,0},{20,4},{24,8},{28,12},{1,17},{... | collective-permute-start | bytes 1179656 | tf_op jit(solution)/shard_map/ppermute | solution.py:124
  (112 other events, 675.3 us)

commit v2 on v1

v2 whole, which is shorter than its diff:
```python
import functools
import math

import jax
import jax.numpy as jnp
from jax import lax
from jax.experimental import pallas as pl
from jax.experimental.pallas import tpu as pltpu
from jax.sharding import PartitionSpec as P

EPS = 1e-06
THETA = 1000000.0
NEGATIVE = -1e30


def layout(lengths, groups, group, slots):
    count = lengths.shape[0]
    mine = groups == group
    sizes_here = jnp.where(mine, lengths, 0)
    starts = jnp.cumsum(sizes_here) - sizes_here
    place = lax.broadcasted_iota(jnp.int32, (slots, count), 0)
    number = lax.broadcasted_iota(jnp.int32, (slots, count), 1)
    inside = mine[None, :] & (place >= starts[None, :]) & (place < (starts + sizes_here)[None, :])
    found = jnp.sum(inside.astype(jnp.int32), axis=1)
    segment = jnp.sum(jnp.where(inside, number, 0), axis=1)
    spot = lax.broadcasted_iota(jnp.int32, (slots,), 0)
    segment = jnp.where(found > 0, segment, count + spot)
    position = jnp.sum(jnp.where(inside, place - starts[None, :], 0), axis=1)
    return (segment, position)


def product(left, right):
    return jnp.dot(left, right, preferred_element_type=jnp.float32)


def contract_rows(left, right):
    return lax.dot_general(
        left, right, (((0,), (0,)), ((), ())), preferred_element_type=jnp.float32
    )


def contract_cols(left, right):
    return lax.dot_general(
        left, right, (((1,), (1,)), ((), ())), preferred_element_type=jnp.float32
    )


VMEM_BYTES = 44 * 1024 * 1024


def local_call(body, shapes, *operands):
    return pl.pallas_call(
        body,
        out_shape=[jax.ShapeDtypeStruct(shape, dtype) for shape, dtype in shapes],
        in_specs=[pl.BlockSpec(memory_space=pltpu.VMEM)] * len(operands),
        out_specs=[pl.BlockSpec(memory_space=pltpu.VMEM)] * len(shapes),
        compiler_params=pltpu.CompilerParams(vmem_limit_bytes=VMEM_BYTES),
    )(*operands)


def half_turn(value_rows):
    return pltpu.roll(value_rows, value_rows.shape[1] // 2, 1)


def head_scale(value_rows):
    return lax.rsqrt(jnp.mean(value_rows * value_rows, axis=1, keepdims=True) + EPS)


def head_cols(index, size):
    return slice(index * size, (index + 1) * size)


def softmax_rows(query, key, allowed, scale):
    scores = jnp.where(allowed, contract_cols(query, key) * scale, NEGATIVE)
    exponent = jnp.exp(scores - jnp.max(scores, axis=1, keepdims=True))
    return exponent / jnp.sum(exponent, axis=1, keepdims=True)


def attention_kernel(
    query_heads,
    key_heads,
    x_own_ref,
    x_other_ref,
    gain_own_ref,
    gain_other_ref,
    keep_ref,
    other_ref,
    gain_query_ref,
    gain_key_ref,
    cosine_ref,
    sine_ref,
    allowed_ref,
    normed_ref,
    inverse_ref,
    sums_ref,
    low_ref,
    attended_ref,
):
    size = gain_query_ref.shape[1]
    scale = 1.0 / math.sqrt(size)
    own = x_own_ref[...].astype(jnp.float32)
    other = x_other_ref[...].astype(jnp.float32)
    total = jnp.sum(own * own, axis=1, keepdims=True) + jnp.sum(
        other * other, axis=1, keepdims=True
    )
    inverse = lax.rsqrt(total / (2 * own.shape[1]) + EPS)
    inverse_ref[...] = inverse
    normed = (own * inverse * gain_own_ref[...]).astype(jnp.bfloat16)
    normed_ref[...] = normed
    normed_other = (other * inverse * gain_other_ref[...]).astype(jnp.bfloat16)
    sums_ref[...] = product(normed, keep_ref[...]) + product(normed_other, other_ref[...])
    cosine, sine = cosine_ref[...], sine_ref[...]
    for head in range(query_heads + key_heads):
        cols = head_cols(head, size)
        gain = gain_query_ref[...] if head < query_heads else gain_key_ref[...]
        one = sums_ref[:, cols]
        one = one * head_scale(one) * gain
        low_ref[:, cols] = (one * cosine + half_turn(one) * sine).astype(jnp.bfloat16)
    values = slice((query_heads + key_heads) * size, (query_heads + 2 * key_heads) * size)
    low_ref[:, values] = sums_ref[:, values].astype(jnp.bfloat16)
    allowed = allowed_ref[...] > 0.0
    share = query_heads // key_heads
    for head in range(query_heads):
        key = low_ref[:, head_cols(query_heads + head // share, size)]
        value = low_ref[:, head_cols(query_heads + key_heads + head // share, size)]
        cols = head_cols(head, size)
        probs = softmax_rows(low_ref[:, cols], key, allowed, scale)
        attended_ref[:, cols] = product(probs.astype(jnp.bfloat16), value).astype(jnp.bfloat16)


def attention_back_kernel(
    query_heads,
    key_heads,
    back_own_ref,
    back_other_ref,
    output_own_ref,
    output_other_ref,
    sums_ref,
    low_ref,
    gain_query_ref,
    gain_key_ref,
    cosine_ref,
    sine_ref,
    allowed_ref,
    pre_ref,
    gain_query_grad_ref,
    gain_key_grad_ref,
):
    size = gain_query_ref.shape[1]
    scale = 1.0 / math.sqrt(size)
    grad = (
        contract_cols(back_own_ref[...], output_own_ref[...])
        + contract_cols(back_other_ref[...], output_other_ref[...])
    ).astype(jnp.bfloat16)
    cosine, sine = cosine_ref[...], sine_ref[...]
    allowed = allowed_ref[...] > 0.0
    share = query_heads // key_heads

    def pull(rotated, head, gain):
        cols = head_cols(head, size)
        turned = rotated * cosine - half_turn(rotated) * sine
        one = sums_ref[:, cols]
        ratio = head_scale(one)
        weighted = turned * gain
        mean = jnp.mean(weighted * one, axis=1, keepdims=True)
        pre_ref[:, cols] = (ratio * weighted - one * ratio**3 * mean).astype(jnp.bfloat16)
        return jnp.sum(turned * one * ratio, axis=0, keepdims=True)

    gain_query_grad = jnp.zeros((1, size), jnp.float32)
    gain_key_grad = jnp.zeros((1, size), jnp.float32)
    for pair in range(key_heads):
        key = low_ref[:, head_cols(query_heads + pair, size)]
        value = low_ref[:, head_cols(query_heads + key_heads + pair, size)]
        key_rotated = jnp.zeros((key.shape[0], size), jnp.float32)
        value_grad = jnp.zeros((key.shape[0], size), jnp.float32)
        for head in range(pair * share, (pair + 1) * share):
            query = low_ref[:, head_cols(head, size)]
            grad_head = grad[:, head_cols(head, size)]
            probs = softmax_rows(query, key, allowed, scale)
            prob_grad = contract_cols(grad_head, value)
            inner = jnp.sum(probs * prob_grad, axis=1, keepdims=True)
            score_grad = (probs * (prob_grad - inner)).astype(jnp.bfloat16)
            gain_query_grad += pull(product(score_grad, key) * scale, head, gain_query_ref[...])
            key_rotated += contract_rows(score_grad, query)
            value_grad += contract_rows(probs.astype(jnp.bfloat16), grad_head)
        gain_key_grad += pull(key_rotated * scale, query_heads + pair, gain_key_ref[...])
        pre_ref[:, head_cols(query_heads + key_heads + pair, size)] = value_grad.astype(
            jnp.bfloat16
        )
    gain_query_grad_ref[...] = gain_query_grad
    gain_key_grad_ref[...] = gain_key_grad


def feed_forward_kernel(
    hidden_ref,
    other_ref,
    gain_own_ref,
    gain_other_ref,
    keep_ref,
    swapped_ref,
    act_grad_ref,
    normed_ref,
    inverse_ref,
    activated_ref,
    grads_ref,
):
    hidden = hidden_ref[...]
    other = other_ref[...].astype(jnp.float32)
    total = jnp.sum(hidden * hidden, axis=1, keepdims=True) + jnp.sum(
        other * other, axis=1, keepdims=True
    )
    inverse = lax.rsqrt(total / (2 * hidden.shape[1]) + EPS)
    inverse_ref[...] = inverse
    normed = (hidden * inverse * gain_own_ref[...]).astype(jnp.bfloat16)
    normed_ref[...] = normed
    normed_other = (other * inverse * gain_other_ref[...]).astype(jnp.bfloat16)
    units = activated_ref.shape[1]
    step = 256
    for start in range(0, units, step):
        low, high = slice(start, start + step), slice(units + start, units + start + step)
        gate = product(normed, keep_ref[:, low]) + product(normed_other, swapped_ref[:, low])
        up = product(normed, keep_ref[:, high]) + product(normed_other, swapped_ref[:, high])
        sigmoid = jax.nn.sigmoid(gate)
        silu = gate * sigmoid
        activated_ref[:, low] = (silu * up).astype(jnp.bfloat16)
        act_grad = act_grad_ref[:, low]
        grads_ref[:, low] = (act_grad * up * sigmoid * (1.0 + gate * (1.0 - sigmoid))).astype(
            jnp.bfloat16
        )
        grads_ref[:, high] = (act_grad * silu).astype(jnp.bfloat16)


def swap(value, axis):
    return lax.ppermute(value, axis, [(0, 1), (1, 0)])


def flip(value, axis, bit):
    size = lax.axis_size(axis)
    return lax.ppermute(value, axis, [(i, i ^ bit) for i in range(size)])


def relative_order(size):
    bits = size.bit_length() - 1
    return [int(format(k, "b").zfill(bits)[::-1], 2) if bits else 0 for k in range(size)]


def relative_blocks(value_rows, axis):
    size = lax.axis_size(axis)
    me = lax.axis_index(axis)
    width = value_rows.shape[1] // size
    turned = value_rows.T.reshape(size, width, value_rows.shape[0])
    parts = [
        lax.dynamic_index_in_dim(turned, me ^ j, 0, keepdims=False) for j in relative_order(size)
    ]
    return jnp.concatenate(parts, axis=0)


def first_half(left, axis):
    blocks = relative_blocks(left, axis)
    half = blocks.shape[0] // 2
    return blocks[:half], flip(blocks[half:], axis, 1)


def scattered_sum(kept, axis):
    bit = 2
    while bit < lax.axis_size(axis):
        half = kept.shape[0] // 2
        arrived = flip(kept[half:].astype(jnp.bfloat16), axis, bit)
        kept = kept[:half] + arrived.astype(jnp.float32)
        bit *= 2
    return kept


def pair_product(halves, right, right_arrived):
    return product(halves[0], right) + product(halves[1], right_arrived)


def total_over(value, axis):
    size = lax.axis_size(axis)
    bit = 1
    while bit < size:
        value = value + flip(value, axis, bit)
        bit *= 2
    return value


def pick(value, index, dim):
    half = value.shape[dim] // 2
    return lax.dynamic_slice_in_dim(value, index * half, half, dim)


def shards(
    tokens,
    cotangent,
    w_query,
    key_weight,
    value_weight,
    w_output,
    w_gate,
    w_up,
    w_down,
    gain_attn,
    gain_query,
    gain_key,
    gain_mlp,
    seq_lengths,
    seq_groups,
):
    half_rows, columns = tokens.shape
    width = columns * 2
    group_rows = half_rows * 2
    head_dim = gain_query.shape[0]
    row = lax.axis_index("row")
    col = lax.axis_index("col")
    mine, theirs = col, 1 - col
    low = jnp.bfloat16

    def exchange_tokens(local):
        own = jnp.concatenate([local, swap(local, "row")], axis=0)
        return own, swap(own, "col")

    x_own_low, x_other_low = exchange_tokens(tokens)
    gains_own = jnp.stack([gain_attn, gain_mlp])
    gains_other = swap(gains_own, "col")
    qkv_keep = jnp.concatenate(
        [pick(w_query, mine, 1), pick(key_weight, mine, 1), pick(value_weight, mine, 1)], axis=1
    )
    qkv_other = swap(
        jnp.concatenate(
            [pick(w_query, theirs, 1), pick(key_weight, theirs, 1), pick(value_weight, theirs, 1)],
            axis=1,
        ),
        "col",
    )
    mlp_keep = jnp.concatenate([pick(w_gate, mine, 1), pick(w_up, mine, 1)], axis=1)
    mlp_theirs = jnp.concatenate([pick(w_gate, theirs, 1), pick(w_up, theirs, 1)], axis=1)
    mlp_other = swap(mlp_theirs, "col")
    output_mine, output_theirs = pick(w_output, mine, 0), pick(w_output, theirs, 0)
    output_other = swap(output_theirs, "col")
    down_mine, down_theirs = pick(w_down, mine, 0), pick(w_down, theirs, 0)
    down_other = swap(down_theirs, "col")
    cot_own, cot_other = exchange_tokens(cotangent)

    segment, position = layout(seq_lengths, seq_groups, lax.axis_index("dp"), group_rows)

    def own_first(vector):
        return jnp.where(row == 0, vector, jnp.roll(vector, half_rows))

    spot = own_first(lax.iota(jnp.int32, group_rows))
    segment, position = own_first(segment), own_first(position)
    allowed = (segment[:, None] == segment[None, :]) & (spot[None, :] <= spot[:, None])

    x_own = x_own_low.astype(jnp.float32)
    query_wide = w_query.shape[1] // 2
    key_wide = key_weight.shape[1] // 2
    query_heads = query_wide // head_dim
    key_heads = key_wide // head_dim
    half = head_dim // 2
    freq = THETA ** (-(jnp.arange(half, dtype=jnp.float32) * 2.0 / head_dim))
    angle = position.astype(jnp.float32)[:, None] * freq[None, :]
    cosine, sine = jnp.cos(angle), jnp.sin(angle)
    cosine = jnp.concatenate([cosine, cosine], axis=1)
    sine = jnp.concatenate([-sine, sine], axis=1)
    allowed = allowed.astype(jnp.float32)
    turns = (gain_query[None, :], gain_key[None, :], cosine, sine, allowed)
    wide = qkv_keep.shape[1]
    normed_own, inverse_attn, sums, heads_low, attended_own = local_call(
        functools.partial(attention_kernel, query_heads, key_heads),
        [
            ((group_rows, columns), low),
            ((group_rows, 1), jnp.float32),
            ((group_rows, wide), jnp.float32),
            ((group_rows, wide), low),
            ((group_rows, query_wide), low),
        ],
        x_own_low,
        x_other_low,
        gains_own[:1],
        gains_other[:1],
        qkv_keep,
        qkv_other,
        *turns,
    )
    attended_other = swap(attended_own, "col")
    cot_flipped = flip(cot_own, "dp", 1)
    normed_halves = first_half(normed_own, "dp")

    def whole(own, other, dim):
        first = jnp.where(col == 0, own, other)
        second = jnp.where(col == 0, other, own)
        return jnp.concatenate([first, second], axis=dim)

    def both_rows(partial_value):
        arrived = swap(partial_value.astype(low), "row").astype(jnp.float32)
        return partial_value + jnp.concatenate(
            [arrived[half_rows:], arrived[:half_rows]], axis=0
        )

    attended_halves = first_half(whole(attended_own, attended_other, 1), "dp")
    partial_out = product(attended_own, output_mine) + product(attended_other, output_theirs)
    hidden = x_own + both_rows(partial_out)
    hidden_low_other = swap(hidden.astype(low), "col")
    hidden_other = hidden_low_other.astype(jnp.float32)
    act_grad = contract_cols(cot_own, down_mine) + contract_cols(cot_other, down_other)
    units = act_grad.shape[1]
    mlp_own, inverse_mlp, activated_own, grads_own = local_call(
        feed_forward_kernel,
        [
            ((group_rows, columns), low),
            ((group_rows, 1), jnp.float32),
            ((group_rows, units), low),
            ((group_rows, 2 * units), low),
        ],
        hidden,
        hidden_low_other,
        gains_own[1:],
        gains_other[1:],
        mlp_keep,
        mlp_other,
        act_grad,
    )
    mlp_halves = first_half(mlp_own, "dp")
    activated_other = swap(activated_own, "col")
    activated_halves = first_half(whole(activated_own, activated_other, 1), "dp")
    grads_other = swap(grads_own, "col")
    mlp_partial = contract_cols(grads_own, mlp_keep) + contract_cols(grads_other, mlp_theirs)
    normed_mlp_grad = both_rows(mlp_partial)
    grads_flipped = flip(grads_own, "dp", 1)
    grads_flipped_other = swap(grads_flipped, "col")
    grad_other = swap(normed_mlp_grad.astype(low), "col").astype(jnp.float32)
    scaled_own = normed_mlp_grad * gains_own[1]
    scaled_other = grad_other * gains_other[1]
    inner = (
        jnp.sum(scaled_own * hidden, axis=1) + jnp.sum(scaled_other * hidden_other, axis=1)
    )[:, None] / width
    cube = inverse_mlp**3 * inner
    hidden_grad = cot_own.astype(jnp.float32) + inverse_mlp * scaled_own - hidden * cube
    hidden_grad_other = (
        cot_other.astype(jnp.float32) + inverse_mlp * scaled_other - hidden_other * cube
    )
    gain_mlp_part = jnp.sum(
        (normed_mlp_grad * hidden * inverse_mlp)[:half_rows], axis=0
    )
    back_own = hidden_grad.astype(low)
    back_other = hidden_grad_other.astype(low)
    back_flipped = flip(back_own, "dp", 1)
    pre_own, gain_query_part, gain_key_part = local_call(
        functools.partial(attention_back_kernel, query_heads, key_heads),
        [
            ((group_rows, wide), low),
            ((1, head_dim), jnp.float32),
            ((1, head_dim), jnp.float32),
        ],
        back_own,
        back_other,
        output_mine,
        output_other,
        sums,
        heads_low,
        *turns,
    )
    pre_other = swap(pre_own, "col")

    pre_flipped = flip(pre_own, "dp", 1)
    pre_flipped_other = swap(pre_flipped, "col")
    qkv_theirs = jnp.concatenate(
        [pick(w_query, theirs, 1), pick(key_weight, theirs, 1), pick(value_weight, theirs, 1)],
        axis=1,
    )
    attn_partial = contract_cols(pre_own, qkv_keep) + contract_cols(pre_other, qkv_theirs)
    arrived = swap(attn_partial[half_rows:].astype(low), "row")
    normed_attn_grad = attn_partial[:half_rows] + arrived.astype(jnp.float32)
    x_mine = x_own[:half_rows]
    inverse_mine = inverse_attn[:half_rows]
    scaled = normed_attn_grad * gain_attn
    dot = jnp.sum(scaled * x_mine, axis=1).reshape(1, half_rows)
    dot = ((dot + swap(dot, "col")) / width).reshape(half_rows, 1)
    input_grad = (
        hidden_grad[:half_rows] + inverse_mine * scaled - x_mine * inverse_mine**3 * dot
    )
    gain_attn_part = jnp.sum(normed_attn_grad * x_mine * inverse_mine, axis=0)

    down_partial = product(activated_own, down_mine) + product(activated_other, down_theirs)
    mixed = (
        hidden[:half_rows]
        + down_partial[:half_rows]
        + swap(down_partial[half_rows:].astype(low), "row").astype(jnp.float32)
    ).astype(low)

    def woven(own, other, widths):
        first = jnp.where(col == 0, own, other)
        second = jnp.where(col == 0, other, own)
        parts, place = [], 0
        for size in widths:
            parts += [first[:, place : place + size], second[:, place : place + size]]
            place += size
        return jnp.concatenate(parts, axis=1)

    mlp_widths = (units, units)
    qkv_widths = (query_wide, key_wide, key_wide)
    mlp_total = scattered_sum(
        pair_product(
            mlp_halves,
            woven(grads_own, grads_other, mlp_widths),
            woven(grads_flipped, grads_flipped_other, mlp_widths),
        ),
        "dp",
    )
    down_total = scattered_sum(pair_product(activated_halves, cot_own, cot_flipped), "dp")
    output_total = scattered_sum(pair_product(attended_halves, back_own, back_flipped), "dp")
    qkv_total = scattered_sum(
        pair_product(
            normed_halves,
            woven(pre_own, pre_other, qkv_widths),
            woven(pre_flipped, pre_flipped_other, qkv_widths),
        ),
        "dp",
    )
    edge = 2 * query_wide
    step = 2 * key_wide

    small = jnp.concatenate([gain_attn_part, gain_mlp_part, gain_query_part[0], gain_key_part[0]])
    small = small.reshape(-1, 128)
    small = total_over(total_over(small, "dp"), "row").reshape(-1)
    heads_part = small[2 * columns :]
    heads_part = heads_part + swap(heads_part, "col")
    return (
        mixed,
        input_grad,
        qkv_total[:, :edge],
        qkv_total[:, edge : edge + step],
        qkv_total[:, edge + step :],
        output_total,
        mlp_total[:, : 2 * units],
        mlp_total[:, 2 * units :],
        down_total,
        small[:columns],
        heads_part[:head_dim],
        heads_part[head_dim:],
        small[columns : 2 * columns],
    )


def solution(mesh):
    in_specs = (
        P(("dp", "row"), "col"),
        P(("dp", "row"), "col"),
        P("col", "row"),
        P("col", "row"),
        P("col", "row"),
        P("row", "col"),
        P("col", "row"),
        P("col", "row"),
        P("row", "col"),
        P("col"),
        P(),
        P(),
        P("col"),
        P(),
        P(),
    )
    out_specs = (
        P(("dp", "row"), "col"),
        P(("dp", "row"), "col"),
        P(("col", "dp"), "row"),
        P(("col", "dp"), "row"),
        P(("col", "dp"), "row"),
        P(("row", "dp"), "col"),
        P(("col", "dp"), "row"),
        P(("col", "dp"), "row"),
        P(("row", "dp"), "col"),
        P("col"),
        P(),
        P(),
        P("col"),
    )
    return jax.shard_map(shards, mesh=mesh, in_specs=in_specs, out_specs=out_specs, check_vma=False)
```

time: 262 us -> 224 us (0.85)
  waiting for transfers between devices: 108 us -> 89.6 us
  matrix products: 39.2 us -> 22.4 us
  other arithmetic: 38 us -> 24.2 us
  Pallas kernels: 0 us -> 11.6 us
  local copies, waits for them, and re-layouts: 40.9 us -> 34.5 us
  starting transfers between devices: 32.6 us -> 38.2 us
    pallas_call x0 -> x3, Pallas kernels: none -> 11.6 us  [local_call(): pl.pallas_call(body, out_shape=[jax.ShapeDtypeStruct(shape, dtype) for sh...]
    ppermute x16 -> x20, waiting for transfers between devices: 94 us -> 83.9 us  [flip(): return lax.ppermute(value, axis, [(i, i ^ bit) for i in range(size)])]
    ppermute x21 -> x23, waiting for transfers between devices: 13.8 us -> 5.73 us  [swap(): return lax.ppermute(value, axis, [(0, 1), (1, 0)])]
    dot_general x5 -> x0, matrix products: 6.77 us -> none  [the longest x1 2.43 us: attend_back(): jnp.einsum('hgqk,qhgd->khd', probs.astype(jnp.bfloat16), grad_grouped, pr...]
    unnamed x206 -> x160, local copies, waits for them, and re-layouts: 4.66 us -> 9.91 us
    ppermute x16 -> x20, starting transfers between devices: 22.1 us -> 27.3 us  [flip(): return lax.ppermute(value, axis, [(i, i ^ bit) for i in range(size)])]
    reduce_sum x9 -> x1, other arithmetic: 5.01 us -> 0.1 us  [layout(): found = jnp.sum(inside.astype(jnp.int32), axis=1)]
    dot_general x16 -> x12, matrix products: 17.1 us -> 12.9 us  [product(): return jnp.dot(left, right, preferred_element_type=jnp.float32)]
  transfers between devices with their start and end apart: 37 -> 43, of which waited for: 14 -> 17; matrix products, arithmetic and copies ran while one was open for 44% -> 31% of each run, Pallas kernels for 0% -> 5%
where the time goes in v2:
time: 224 us; the launch traced here: 223 us
  waiting for transfers between devices  89.6 us (40%)
  starting transfers between devices  38.2 us (17%)
  local copies, waits for them, and re-layouts  34.5 us (15%)
  other arithmetic  24.2 us (11%)
  matrix products  22.4 us (10%)
  Pallas kernels  11.6 us (5%)
    ppermute x20, waiting for transfers between devices, flip(): return lax.ppermute(value, axis, [(i, i ^ bit) for i in range(size)])  83.9 us
    ppermute x20, starting transfers between devices, flip(): return lax.ppermute(value, axis, [(i, i ^ bit) for i in range(size)])  27.3 us
    dot_general x12, matrix products, product(): return jnp.dot(left, right, preferred_element_type=jnp.float32)  12.9 us
    pallas_call x3, Pallas kernels, local_call(): pl.pallas_call(body, out_shape=[jax.ShapeDtypeStruct(shape, dtype) for sh...  11.6 us
    ppermute x23, starting transfers between devices, swap(): return lax.ppermute(value, axis, [(0, 1), (1, 0)])  10.9 us
    unnamed x160, local copies, waits for them, and re-layouts  9.91 us
    dot_general x6, matrix products, contract_cols(): lax.dot_general(left, right, (((1,), (1,)), ((), ())), preferred_element_...  9.54 us
    dynamic_slice x5, local copies, waits for them, and re-layouts, pick(): return lax.dynamic_slice_in_dim(value, index * half, half, dim)  7.49 us
  transfers between devices with their start and end apart: 43, of which 17 were waited for; matrix products, arithmetic and copies ran while one was open for 31% of the time, Pallas kernels for 5%

profile of v2, /device:TPU:0, one launch (start us, length us, event | category | flops | bytes accessed | tf_op | source)
XLA Modules:
  0.0 222.6 jit_solution(1001841122260167600)
XLA Ops:
  4.7 2.5 %collective-permute-start = (bf16[128,512]{1,0:T(8,128)(2,1)}, bf16[128,512]{1,0:T(8,128)(2,1)}, u32[]{:S(2)}, u32[]{:S(2)}) collective-permute-start(bf16[128,512]{1,0:T(8,128)(2,1)} %param.15), channel_id=1, source_target_pairs={{0,2},{2,0},{1,3},{3,1},{4,6},{6,4},{5,7},{7,5},{8,10},{10,8},{9,1... | collective-permute-start | bytes 393224 | tf_op jit(solution)/shard_map/ppermute | solution.py:234
  12.2 2.2 constant_dynamic-slice_fusion.1
  19.0 2.1 constant_dynamic-slice_fusion.6
  31.8 4.0 %shard_map.246 = (bf16[256,512]{1,0:T(8,128)(2,1)S(1)}, f32[256,1]{1,0:T(8,128)S(1)}, f32[256,1024]{1,0:T(8,128)S(1)}, bf16[256,1024]{1,0:T(8,128)(2,1)S(1)}, bf16[256,512]{1,0:T(8,128)(2,1)S(1)}) custom-call(bf16[256,512]{1,0:T(8,128)(2,1)S(1)} %constant_dynamic-update-slice_fusion.x_own_ref, bf16[256,512]{1,0:T(8,128)(2,1)S(1)} %collective-permute-done.1.x_other_ref, ...), custom_call_target="tpu_custom_call" | custom-call | tf_op jit(solution)/shard_map/pallas_call | solution.py:52
  37.7 2.4 %convolution_add_fusion.4.act_grad_ref = f32[256,768]{1,0:T(8,128)} fusion(f32[256,768]{1,0:T(8,128)S(1)} %fusion.94, bf16[256,512]{1,0:T(8,128)(2,1)} %constant_dynamic-update-slice_fusion.2, bf16[1536,512]{1,0:T(8,128)(2,1)S(1)} %copy-done, s32[]{:T(128)S(6)} %select_n.215), kind=kOutput, calls=%fused_computation.23 | convolution fusion | flops 201523200 | bytes 2621444 | tf_op jit(solution)/shard_map/dot_general | solution.py:43
  46.8 4.6 %collective-permute-done.5 = bf16[256,512]{1,0:T(8,128)(2,1)S(1)} collective-permute-done((bf16[256,512]{1,0:T(8,128)(2,1)S(1)}, bf16[256,512]{1,0:T(8,128)(2,1)S(1)}, u32[]{:S(2)}, u32[]{:S(2)}) %collective-permute-start.5) | collective-permute-done | bytes 262176 | tf_op jit(solution)/shard_map/ppermute | solution.py:234
  56.7 3.7 %shard_map.247 = (bf16[256,512]{1,0:T(8,128)(2,1)S(1)}, f32[256,1]{1,0:T(8,128)S(1)}, bf16[256,768]{1,0:T(8,128)(2,1)}, bf16[256,1536]{1,0:T(8,128)(2,1)}) custom-call(f32[256,512]{1,0:T(8,128)S(1)} %get-tuple-element.51.hidden_ref, bf16[256,512]{1,0:T(8,128)(2,1)} %collective-permute-done.6.other_ref, f32[1,512]{1,0:T(1,128)S(1)} %bitcast.130, ...), custom_call_target="tpu_custom_call" | custom-call | tf_op jit(solution)/shard_map/pallas_call | solution.py:52
  78.9 5.6 %collective-permute-done.34 = bf16[768,256]{1,0:T(8,128)(2,1)S(1)} collective-permute-done((bf16[768,256]{1,0:T(8,128)(2,1)S(1)}, bf16[768,256]{1,0:T(8,128)(2,1)S(1)}, u32[]{:S(2)}, u32[]{:S(2)}) %collective-permute-start.34) | collective-permute-done | bytes 393248 | tf_op jit(solution)/shard_map/ppermute | solution.py:239
  94.2 8.2 %collective-permute-done.36 = bf16[384,512]{1,0:T(8,128)(2,1)S(1)} collective-permute-done((bf16[384,512]{1,0:T(8,128)(2,1)S(1)}, bf16[384,512]{1,0:T(8,128)(2,1)S(1)}, u32[]{:S(2)}, u32[]{:S(2)}) %collective-permute-start.36) | collective-permute-done | bytes 393248 | tf_op jit(solution)/shard_map/ppermute | solution.py:239
  110.1 4.0 %shard_map.248 = (bf16[256,1024]{1,0:T(8,128)(2,1)S(1)}, f32[1,128]{1,0:T(1,128)S(1)}, f32[1,128]{1,0:T(1,128)S(1)}) custom-call(bf16[256,512]{1,0:T(8,128)(2,1)S(1)} %get-tuple-element.46.back_own_ref, bf16[256,512]{1,0:T(8,128)(2,1)S(1)} %get-tuple-element.132.back_other_ref, bf16[512,512]{1,0:T(8,128)(2,1)S(1)} %get-tuple-element.66.output_own_ref, ...), custom_call_target="tpu_custom_call" | custom-call | tf_op jit(solution)/shard_map/pallas_call | solution.py:52
  114.8 2.6 %collective-permute-start.37 = (bf16[192,512]{1,0:T(8,128)(2,1)S(1)}, bf16[192,512]{1,0:T(8,128)(2,1)S(1)}, u32[]{:S(2)}, u32[]{:S(2)}) collective-permute-start(bf16[192,512]{1,0:T(8,128)(2,1)S(1)} %copy-done.60), channel_id=1, source_target_pairs={{0,16},{4,20},{8,24},{12,28},{16,0},{20,4},{24,8},{28,12},{1,17},{... | collective-permute-start | bytes 589832 | tf_op jit(solution)/shard_map/ppermute | solution.py:239
  118.1 8.2 %collective-permute-done.37 = bf16[192,512]{1,0:T(8,128)(2,1)S(1)} collective-permute-done((bf16[192,512]{1,0:T(8,128)(2,1)S(1)}, bf16[192,512]{1,0:T(8,128)(2,1)S(1)}, u32[]{:S(2)}, u32[]{:S(2)}) %collective-permute-start.37) | collective-permute-done | bytes 196640 | tf_op jit(solution)/shard_map/ppermute | solution.py:239
  141.2 3.6 %collective-permute-done.21 = bf16[256,1024]{1,0:T(8,128)(2,1)S(1)} collective-permute-done((bf16[256,1024]{1,0:T(8,128)(2,1)S(1)}, bf16[256,1024]{1,0:T(8,128)(2,1)S(1)}, u32[]{:S(2)}, u32[]{:S(2)}) %collective-permute-start.21) | collective-permute-done | bytes 524320 | tf_op jit(solution)/shard_map/ppermute | solution.py:239
  145.6 13.1 %collective-permute-done.27 = bf16[256,512]{1,0:T(8,128)(2,1)S(1)} collective-permute-done((bf16[256,512]{1,0:T(8,128)(2,1)S(1)}, bf16[256,512]{1,0:T(8,128)(2,1)S(1)}, u32[]{:S(2)}, u32[]{:S(2)}) %collective-permute-start.27) | collective-permute-done | bytes 262176 | tf_op jit(solution)/shard_map/ppermute | solution.py:239
  158.8 2.4 %collective-permute-start.28 = (bf16[128,512]{1,0:T(8,128)(2,1)S(1)}, bf16[128,512]{1,0:T(8,128)(2,1)S(1)}, u32[]{:S(2)}, u32[]{:S(2)}) collective-permute-start(bf16[128,512]{1,0:T(8,128)(2,1)S(1)} %slice.438), channel_id=1, source_target_pairs={{0,16},{4,20},{8,24},{12,28},{16,0},{20,4},{24,8},{28,12},{1,17},{... | collective-permute-start | bytes 393224 | tf_op jit(solution)/shard_map/ppermute | solution.py:239
  161.2 6.2 %collective-permute-done.28 = bf16[128,512]{1,0:T(8,128)(2,1)S(1)} collective-permute-done((bf16[128,512]{1,0:T(8,128)(2,1)S(1)}, bf16[128,512]{1,0:T(8,128)(2,1)S(1)}, u32[]{:S(2)}, u32[]{:S(2)}) %collective-permute-start.28) | collective-permute-done | bytes 131104 | tf_op jit(solution)/shard_map/ppermute | solution.py:239
  168.8 2.3 %collective-permute-done.39 = f32[10,128]{1,0:T(8,128)S(1)} collective-permute-done((f32[10,128]{1,0:T(8,128)S(1)}, f32[10,128]{1,0:T(8,128)S(1)}, u32[]{:S(2)}, u32[]{:S(2)}) %collective-permute-start.39) | collective-permute-done | bytes 5152 | tf_op jit(solution)/shard_map/ppermute | solution.py:239
  171.0 2.1 collective-permute-start.40
  173.1 2.5 %collective-permute-done.40 = f32[10,128]{1,0:T(8,128)S(1)} collective-permute-done((f32[10,128]{1,0:T(8,128)S(1)}, f32[10,128]{1,0:T(8,128)S(1)}, u32[]{:S(2)}, u32[]{:S(2)}) %collective-permute-start.40) | collective-permute-done | bytes 5152 | tf_op jit(solution)/shard_map/ppermute | solution.py:239
  181.5 2.1 collective-permute-start.33
  185.5 2.1 collective-permute-start.23
  187.6 14.6 %collective-permute-done.33 = bf16[64,3072]{1,0:T(8,128)(2,1)S(1)} collective-permute-done((bf16[64,3072]{1,0:T(8,128)(2,1)S(1)}, bf16[64,3072]{1,0:T(8,128)(2,1)S(1)}, u32[]{:S(2)}, u32[]{:S(2)}) %collective-permute-start.33) | collective-permute-done | bytes 393248 | tf_op jit(solution)/shard_map/ppermute | solution.py:239
  202.3 4.8 %collective-permute-done.23 = bf16[128,2048]{1,0:T(8,128)(2,1)S(1)} collective-permute-done((bf16[128,2048]{1,0:T(8,128)(2,1)S(1)}, bf16[128,2048]{1,0:T(8,128)(2,1)S(1)}, u32[]{:S(2)}, u32[]{:S(2)}) %collective-permute-start.23) | collective-permute-done | bytes 524320 | tf_op jit(solution)/shard_map/ppermute | solution.py:239
  208.7 12.4 %collective-permute-done.24 = bf16[64,2048]{1,0:T(8,128)(2,1)S(1)} collective-permute-done((bf16[64,2048]{1,0:T(8,128)(2,1)S(1)}, bf16[64,2048]{1,0:T(8,128)(2,1)S(1)}, u32[]{:S(2)}, u32[]{:S(2)}) %collective-permute-start.24) | collective-permute-done | bytes 262176 | tf_op jit(solution)/shard_map/ppermute | solution.py:239
  (348 shorter events, 102.4 us)
Async XLA Ops:
  4.3 27.5 %collective-permute-start.3 = (bf16[512,1024]{1,0:T(8,128)(2,1)}, bf16[512,1024]{1,0:T(8,128)(2,1)}, u32[]{:S(2)}, u32[]{:S(2)}) collective-permute-start(bf16[512,1024]{1,0:T(8,128)(2,1)} %pad_maximum_fusion.3), channel_id=1, source_target_pairs={{0,1},{1,0},{2,3},{3,2},{4,5},{5,4},{6,7},{7,6},{8,9},{9,8},{10,11... | collective-permute-start | bytes 3145736 | tf_op jit(solution)/shard_map/ppermute | solution.py:234
  4.7 21.1 %collective-permute-start = (bf16[128,512]{1,0:T(8,128)(2,1)}, bf16[128,512]{1,0:T(8,128)(2,1)}, u32[]{:S(2)}, u32[]{:S(2)}) collective-permute-start(bf16[128,512]{1,0:T(8,128)(2,1)} %param.15), channel_id=1, source_target_pairs={{0,2},{2,0},{1,3},{3,1},{4,6},{6,4},{5,7},{7,5},{8,10},{10,8},{9,1... | collective-permute-start | bytes 393224 | tf_op jit(solution)/shard_map/ppermute | solution.py:234
  7.9 16.3 %collective-permute-start.2 = (f32[2,512]{1,0:T(2,128)}, f32[2,512]{1,0:T(2,128)S(1)}, u32[]{:S(2)}, u32[]{:S(2)}) collective-permute-start(f32[2,512]{1,0:T(2,128)} %pad_maximum_fusion.10), channel_id=1, source_target_pairs={{0,1},{1,0},{2,3},{3,2},{4,5},{5,4},{6,7},{7,6},{8,9},{9,8},{10,11... | collective-permute-start | bytes 12296 | tf_op jit(solution)/shard_map/ppermute | solution.py:234
  9.1 19.2 %collective-permute-start.10 = (bf16[768,512]{1,0:T(8,128)(2,1)}, bf16[768,512]{1,0:T(8,128)(2,1)}, u32[]{:S(2)}, u32[]{:S(2)}) collective-permute-start(bf16[768,512]{1,0:T(8,128)(2,1)} %constant_dynamic-slice_fusion), channel_id=1, source_target_pairs={{0,1},{1,0},{2,3},{3,2},{4,5},{5,4},{6,7},{7,6},{8,9},{9,8},{10,11... | collective-permute-start | bytes 2359304 | tf_op jit(solution)/shard_map/ppermute | solution.py:234
  9.3 13.0 %collective-permute-start.8 = (bf16[128,512]{1,0:T(8,128)(2,1)}, bf16[128,512]{1,0:T(8,128)(2,1)}, u32[]{:S(2)}, u32[]{:S(2)}) collective-permute-start(bf16[128,512]{1,0:T(8,128)(2,1)} %param.16), channel_id=1, source_target_pairs={{0,2},{2,0},{1,3},{3,1},{4,6},{6,4},{5,7},{7,5},{8,10},{10,8},{9,1... | collective-permute-start | bytes 393224 | tf_op jit(solution)/shard_map/ppermute | solution.py:234
  22.4 32.9 %collective-permute-start.7 = (bf16[512,1536]{1,0:T(8,128)(2,1)}, bf16[512,1536]{1,0:T(8,128)(2,1)}, u32[]{:S(2)}, u32[]{:S(2)}) collective-permute-start(bf16[512,1536]{1,0:T(8,128)(2,1)} %pad_maximum_fusion.1), channel_id=1, source_target_pairs={{0,1},{1,0},{2,3},{3,2},{4,5},{5,4},{6,7},{7,6},{8,9},{9,8},{10,11... | collective-permute-start | bytes 4718600 | tf_op jit(solution)/shard_map/ppermute | solution.py:234
  25.8 83.1 %collective-permute-start.16 = (bf16[512,512]{1,0:T(8,128)(2,1)}, bf16[512,512]{1,0:T(8,128)(2,1)}, u32[]{:S(2)}, u32[]{:S(2)}) collective-permute-start(bf16[512,512]{1,0:T(8,128)(2,1)} %get-tuple-element.67), channel_id=1, source_target_pairs={{0,1},{1,0},{2,3},{3,2},{4,5},{5,4},{6,7},{7,6},{8,9},{9,8},{10,11... | collective-permute-start | bytes 1572872 | tf_op jit(solution)/shard_map/ppermute | solution.py:234
  28.2 49.6 %collective-permute-start.35 = (bf16[256,512]{1,0:T(8,128)(2,1)}, bf16[256,512]{1,0:T(8,128)(2,1)}, u32[]{:S(2)}, u32[]{:S(2)}) collective-permute-start(bf16[256,512]{1,0:T(8,128)(2,1)} %constant_dynamic-update-slice_fusion.2), channel_id=1, source_target_pairs={{0,4},{4,0},{8,12},{12,8},{16,20},{20,16},{24,28},{28,24},{1,5},{5... | collective-permute-start | bytes 786440 | tf_op jit(solution)/shard_map/ppermute | solution.py:239
  45.6 138.0 %collective-permute-start.20 = (bf16[256,256]{1,0:T(8,128)(2,1)}, bf16[256,256]{1,0:T(8,128)(2,1)}, u32[]{:S(2)}, u32[]{:S(2)}) collective-permute-start(bf16[256,256]{1,0:T(8,128)(2,1)} %pad_maximum_fusion.8), channel_id=1, source_target_pairs={{0,4},{4,0},{8,12},{12,8},{16,20},{20,16},{24,28},{28,24},{1,5},{5... | collective-permute-start | bytes 393224 | tf_op jit(solution)/shard_map/ppermute | solution.py:239
  63.7 69.7 %collective-permute-start.25 = (bf16[512,256]{1,0:T(8,128)(2,1)}, bf16[512,256]{1,0:T(8,128)(2,1)}, u32[]{:S(2)}, u32[]{:S(2)}) collective-permute-start(bf16[512,256]{1,0:T(8,128)(2,1)} %pad_maximum_fusion.5), channel_id=1, source_target_pairs={{0,4},{4,0},{8,12},{12,8},{16,20},{20,16},{24,28},{28,24},{1,5},{5... | collective-permute-start | bytes 786440 | tf_op jit(solution)/shard_map/ppermute | solution.py:239
  72.6 12.0 %collective-permute-start.34 = (bf16[768,256]{1,0:T(8,128)(2,1)S(1)}, bf16[768,256]{1,0:T(8,128)(2,1)S(1)}, u32[]{:S(2)}, u32[]{:S(2)}) collective-permute-start(bf16[768,256]{1,0:T(8,128)(2,1)S(1)} %pad_maximum_fusion.4), channel_id=1, source_target_pairs={{0,4},{4,0},{8,12},{12,8},{16,20},{20,16},{24,28},{28,24},{1,5},{5... | collective-permute-start | bytes 1179656 | tf_op jit(solution)/shard_map/ppermute | solution.py:239
  77.9 25.6 %collective-permute-start.30 = (bf16[256,1536]{1,0:T(8,128)(2,1)}, bf16[256,1536]{1,0:T(8,128)(2,1)}, u32[]{:S(2)}, u32[]{:S(2)}) collective-permute-start(bf16[256,1536]{1,0:T(8,128)(2,1)} %get-tuple-element.28), channel_id=1, source_target_pairs={{0,4},{4,0},{8,12},{12,8},{16,20},{20,16},{24,28},{28,24},{1,5},{5... | collective-permute-start | bytes 2359304 | tf_op jit(solution)/shard_map/ppermute | solution.py:239
  103.5 25.8 %collective-permute-start.29 = (bf16[256,256]{1,0:T(8,128)(2,1)}, bf16[256,256]{1,0:T(8,128)(2,1)}, u32[]{:S(2)}, u32[]{:S(2)}) collective-permute-start(bf16[256,256]{1,0:T(8,128)(2,1)} %pad_maximum_fusion.9), channel_id=1, source_target_pairs={{0,4},{4,0},{8,12},{12,8},{16,20},{20,16},{24,28},{28,24},{1,5},{5... | collective-permute-start | bytes 393224 | tf_op jit(solution)/shard_map/ppermute | solution.py:239
  105.1 22.6 %collective-permute-start.31 = (bf16[256,1536]{1,0:T(8,128)(2,1)}, bf16[256,1536]{1,0:T(8,128)(2,1)}, u32[]{:S(2)}, u32[]{:S(2)}) collective-permute-start(bf16[256,1536]{1,0:T(8,128)(2,1)} %collective-permute-done.30), channel_id=1, source_target_pairs={{0,1},{1,0},{2,3},{3,2},{4,5},{5,4},{6,7},{7,6},{8,9},{9,8},{10,11... | collective-permute-start | bytes 2359304 | tf_op jit(solution)/shard_map/ppermute | solution.py:234
  114.8 11.5 %collective-permute-start.37 = (bf16[192,512]{1,0:T(8,128)(2,1)S(1)}, bf16[192,512]{1,0:T(8,128)(2,1)S(1)}, u32[]{:S(2)}, u32[]{:S(2)}) collective-permute-start(bf16[192,512]{1,0:T(8,128)(2,1)S(1)} %copy-done.60), channel_id=1, source_target_pairs={{0,16},{4,20},{8,24},{12,28},{16,0},{20,4},{24,8},{28,12},{1,17},{... | collective-permute-start | bytes 589832 | tf_op jit(solution)/shard_map/ppermute | solution.py:239
  129.3 15.5 %collective-permute-start.21 = (bf16[256,1024]{1,0:T(8,128)(2,1)S(1)}, bf16[256,1024]{1,0:T(8,128)(2,1)S(1)}, u32[]{:S(2)}, u32[]{:S(2)}) collective-permute-start(bf16[256,1024]{1,0:T(8,128)(2,1)S(1)} %get-tuple-element.32), channel_id=1, source_target_pairs={{0,4},{4,0},{8,12},{12,8},{16,20},{20,16},{24,28},{28,24},{1,5},{5... | collective-permute-start | bytes 1572872 | tf_op jit(solution)/shard_map/ppermute | solution.py:239
  133.3 47.9 %collective-permute-start.32 = (bf16[128,3072]{1,0:T(8,128)(2,1)S(1)}, bf16[128,3072]{1,0:T(8,128)(2,1)S(1)}, u32[]{:S(2)}, u32[]{:S(2)}) collective-permute-start(bf16[128,3072]{1,0:T(8,128)(2,1)S(1)} %slice.431), channel_id=1, source_target_pairs={{0,8},{4,12},{8,0},{12,4},{16,24},{20,28},{24,16},{28,20},{1,9},{5... | collective-permute-start | bytes 2359304 | tf_op jit(solution)/shard_map/ppermute | solution.py:239
  135.8 22.9 %collective-permute-start.27 = (bf16[256,512]{1,0:T(8,128)(2,1)S(1)}, bf16[256,512]{1,0:T(8,128)(2,1)S(1)}, u32[]{:S(2)}, u32[]{:S(2)}) collective-permute-start(bf16[256,512]{1,0:T(8,128)(2,1)S(1)} %slice.435), channel_id=1, source_target_pairs={{0,8},{4,12},{8,0},{12,4},{16,24},{20,28},{24,16},{28,20},{1,9},{5... | collective-permute-start | bytes 786440 | tf_op jit(solution)/shard_map/ppermute | solution.py:239
  144.8 36.2 %collective-permute-start.22 = (bf16[256,1024]{1,0:T(8,128)(2,1)S(1)}, bf16[256,1024]{1,0:T(8,128)(2,1)S(1)}, u32[]{:S(2)}, u32[]{:S(2)}) collective-permute-start(bf16[256,1024]{1,0:T(8,128)(2,1)S(1)} %collective-permute-done.21), channel_id=1, source_target_pairs={{0,1},{1,0},{2,3},{3,2},{4,5},{5,4},{6,7},{7,6},{8,9},{9,8},{10,11... | collective-permute-start | bytes 1572872 | tf_op jit(solution)/shard_map/ppermute | solution.py:234
  145.0 16.2 %collective-permute-start.38 = (f32[10,128]{1,0:T(8,128)S(1)}, f32[10,128]{1,0:T(8,128)S(1)}, u32[]{:S(2)}, u32[]{:S(2)}) collective-permute-start(f32[10,128]{1,0:T(8,128)S(1)} %maximum_bitcast_fusion.2), channel_id=1, source_target_pairs={{0,4},{4,0},{8,12},{12,8},{16,20},{20,16},{24,28},{28,24},{1,5},{5... | collective-permute-start | bytes 15368 | tf_op jit(solution)/shard_map/ppermute | solution.py:239
  161.2 12.0 %collective-permute-start.19 = (f32[1,128]{1,0:T(1,128)S(1)}, f32[1,128]{1,0:T(1,128)S(1)}, u32[]{:S(2)}, u32[]{:S(2)}) collective-permute-start(f32[1,128]{1,0:T(1,128)S(1)} %bitcast.150), channel_id=1, source_target_pairs={{0,1},{1,0},{2,3},{3,2},{4,5},{5,4},{6,7},{7,6},{8,9},{9,8},{10,11... | collective-permute-start | bytes 1544 | tf_op jit(solution)/shard_map/ppermute | solution.py:234
  181.5 20.7 %collective-permute-start.33 = (bf16[64,3072]{1,0:T(8,128)(2,1)S(1)}, bf16[64,3072]{1,0:T(8,128)(2,1)S(1)}, u32[]{:S(2)}, u32[]{:S(2)}) collective-permute-start(bf16[64,3072]{1,0:T(8,128)(2,1)S(1)} %slice.434), channel_id=1, source_target_pairs={{0,16},{4,20},{8,24},{12,28},{16,0},{20,4},{24,8},{28,12},{1,17},{... | collective-permute-start | bytes 1179656 | tf_op jit(solution)/shard_map/ppermute | solution.py:239
  185.5 21.6 %collective-permute-start.23 = (bf16[128,2048]{1,0:T(8,128)(2,1)S(1)}, bf16[128,2048]{1,0:T(8,128)(2,1)S(1)}, u32[]{:S(2)}, u32[]{:S(2)}) collective-permute-start(bf16[128,2048]{1,0:T(8,128)(2,1)S(1)} %slice.432), channel_id=1, source_target_pairs={{0,8},{4,12},{8,0},{12,4},{16,24},{20,28},{24,16},{28,20},{1,9},{5... | collective-permute-start | bytes 1572872 | tf_op jit(solution)/shard_map/ppermute | solution.py:239
  207.3 13.8 %collective-permute-start.24 = (bf16[64,2048]{1,0:T(8,128)(2,1)S(1)}, bf16[64,2048]{1,0:T(8,128)(2,1)S(1)}, u32[]{:S(2)}, u32[]{:S(2)}) collective-permute-start(bf16[64,2048]{1,0:T(8,128)(2,1)S(1)} %slice.436), channel_id=1, source_target_pairs={{0,16},{4,20},{8,24},{12,28},{16,0},{20,4},{24,8},{28,12},{1,17},{... | collective-permute-start | bytes 786440 | tf_op jit(solution)/shard_map/ppermute | solution.py:239
  (93 other events, 503.1 us)

commit v3 on v2

--- a/solution.py
+++ b/solution.py
@@ -261,24 +261,36 @@
     return blocks[:half], flip(blocks[half:], axis, 1)
 
 
-def scattered_sum(kept, axis):
+def after(value, anchor):
+    return lax.optimization_barrier((value, anchor))[0]
+
+
+def split_half(kept):
+    half = kept.shape[0] // 2
+    return kept[:half], kept[half:].astype(jnp.bfloat16)
+
+
+def scattered_sum(kept, away, axis, anchors):
+    first = kept
     bit = 2
-    while bit < lax.axis_size(axis):
-        half = kept.shape[0] // 2
-        arrived = flip(kept[half:].astype(jnp.bfloat16), axis, bit)
-        kept = kept[:half] + arrived.astype(jnp.float32)
+    size = lax.axis_size(axis)
+    while bit < size:
+        arrived = flip(away, axis, bit)
+        arrived = after(arrived, anchors[0 if bit == 2 else 1])
+        kept = kept + arrived.astype(jnp.float32)
+        first = kept if bit == 2 else first
         bit *= 2
-    return kept
+        if bit < size:
+            kept, away = split_half(kept)
+    return kept, first
 
 
 def pair_product(halves, right, right_arrived):
     return product(halves[0], right) + product(halves[1], right_arrived)
 
 
-def total_over(value, axis):
-    size = lax.axis_size(axis)
-    bit = 1
-    while bit < size:
+def total_over(value, axis, bit=1):
+    while bit < lax.axis_size(axis):
         value = value + flip(value, axis, bit)
         bit *= 2
     return value
@@ -425,6 +437,8 @@
     grads_other = swap(grads_own, "col")
     mlp_partial = contract_cols(grads_own, mlp_keep) + contract_cols(grads_other, mlp_theirs)
     normed_mlp_grad = both_rows(mlp_partial)
+    down_sides = (activated_halves[0], after(activated_halves[1], normed_mlp_grad))
+    down_halves = split_half(pair_product(down_sides, cot_own, cot_flipped))
     grads_flipped = flip(grads_own, "dp", 1)
     grads_flipped_other = swap(grads_flipped, "col")
     grad_other = swap(normed_mlp_grad.astype(low), "col").astype(jnp.float32)
@@ -443,6 +457,24 @@
     )
     back_own = hidden_grad.astype(low)
     back_other = hidden_grad_other.astype(low)
+    qkv_widths = (query_wide, key_wide, key_wide)
+    mlp_widths = (units, units)
+    def woven(own, other, widths):
+        first = jnp.where(col == 0, own, other)
+        second = jnp.where(col == 0, other, own)
+        parts, place = [], 0
+        for size in widths:
+            parts += [first[:, place : place + size], second[:, place : place + size]]
+            place += size
+        return jnp.concatenate(parts, axis=1)
+
+    mlp_product = split_half(
+        pair_product(
+            mlp_halves,
+            woven(grads_own, grads_other, mlp_widths),
+            woven(grads_flipped, grads_flipped_other, mlp_widths),
+        )
+    )
     back_flipped = flip(back_own, "dp", 1)
     pre_own, gain_query_part, gain_key_part = local_call(
         functools.partial(attention_back_kernel, query_heads, key_heads),
@@ -451,7 +483,7 @@
             ((1, head_dim), jnp.float32),
             ((1, head_dim), jnp.float32),
         ],
-        back_own,
+        after(back_own, (mlp_product[1], down_halves[1])),
         back_other,
         output_mine,
         output_other,
@@ -487,41 +519,27 @@
         + swap(down_partial[half_rows:].astype(low), "row").astype(jnp.float32)
     ).astype(low)
 
-    def woven(own, other, widths):
-        first = jnp.where(col == 0, own, other)
-        second = jnp.where(col == 0, other, own)
-        parts, place = [], 0
-        for size in widths:
-            parts += [first[:, place : place + size], second[:, place : place + size]]
-            place += size
-        return jnp.concatenate(parts, axis=1)
-
-    mlp_widths = (units, units)
-    qkv_widths = (query_wide, key_wide, key_wide)
-    mlp_total = scattered_sum(
-        pair_product(
-            mlp_halves,
-            woven(grads_own, grads_other, mlp_widths),
-            woven(grads_flipped, grads_flipped_other, mlp_widths),
-        ),
-        "dp",
-    )
-    down_total = scattered_sum(pair_product(activated_halves, cot_own, cot_flipped), "dp")
-    output_total = scattered_sum(pair_product(attended_halves, back_own, back_flipped), "dp")
-    qkv_total = scattered_sum(
+    down_total, _ = scattered_sum(*down_halves, "dp", (pre_own, input_grad))
+    mlp_total, _ = scattered_sum(*mlp_product, "dp", (attn_partial, input_grad))
+    output_halves = split_half(
+        pair_product(attended_halves, back_own, after(back_flipped, pre_own))
+    )
+    output_total, _ = scattered_sum(*output_halves, "dp", (input_grad, input_grad))
+    qkv_product = split_half(
         pair_product(
             normed_halves,
             woven(pre_own, pre_other, qkv_widths),
             woven(pre_flipped, pre_flipped_other, qkv_widths),
-        ),
-        "dp",
-    )
+        )
+    )
+    qkv_total, qkv_first = scattered_sum(*qkv_product, "dp", (input_grad, input_grad))
     edge = 2 * query_wide
     step = 2 * key_wide
 
     small = jnp.concatenate([gain_attn_part, gain_mlp_part, gain_query_part[0], gain_key_part[0]])
-    small = small.reshape(-1, 128)
-    small = total_over(total_over(small, "dp"), "row").reshape(-1)
+    small = total_over(small.reshape(-1, 128), "row")
+    small = after(small + flip(small, "dp", 1), qkv_first)
+    small = total_over(small, "dp", 2).reshape(-1)
     heads_part = small[2 * columns :]
     heads_part = heads_part + swap(heads_part, "col")
     return (

time: 224 us -> 213 us (0.951)
  waiting for transfers between devices: 89.6 us -> 71.3 us
  local copies, waits for them, and re-layouts: 34.5 us -> 41 us
  other arithmetic: 24.2 us -> 26.9 us
    ppermute x20, waiting for transfers between devices: 83.9 us -> 58.6 us  [flip(): return lax.ppermute(value, axis, [(i, i ^ bit) for i in range(size)])]
    ppermute x23, waiting for transfers between devices: 5.73 us -> 12.7 us  [swap(): return lax.ppermute(value, axis, [(0, 1), (1, 0)])]
    unnamed x160 -> x158, local copies, waits for them, and re-layouts: 9.91 us -> 13.4 us
  transfers between devices with their start and end apart: 43 -> 43, of which waited for: 17 -> 15; matrix products, arithmetic and copies ran while one was open for 31% -> 35% of each run, Pallas kernels for 5% -> 5%
where the time goes in v3:
time: 213 us; the launch traced here: 212 us
  waiting for transfers between devices  71.3 us (33%)
  local copies, waits for them, and re-layouts  41 us (19%)
  starting transfers between devices  39.2 us (18%)
  other arithmetic  26.9 us (13%)
  matrix products  20.2 us (9%)
  Pallas kernels  11.3 us (5%)
    ppermute x20, waiting for transfers between devices, flip(): return lax.ppermute(value, axis, [(i, i ^ bit) for i in range(size)])  58.6 us
    ppermute x20, starting transfers between devices, flip(): return lax.ppermute(value, axis, [(i, i ^ bit) for i in range(size)])  27 us
    unnamed x158, local copies, waits for them, and re-layouts  13.4 us
    ppermute x23, waiting for transfers between devices, swap(): return lax.ppermute(value, axis, [(0, 1), (1, 0)])  12.7 us
    ppermute x23, starting transfers between devices, swap(): return lax.ppermute(value, axis, [(0, 1), (1, 0)])  12.2 us
    dot_general x12, matrix products, product(): return jnp.dot(left, right, preferred_element_type=jnp.float32)  11.9 us
    pallas_call x3, Pallas kernels, local_call(): pl.pallas_call(body, out_shape=[jax.ShapeDtypeStruct(shape, dtype) for sh...  11.3 us
    dot_general x6, matrix products, contract_cols(): lax.dot_general(left, right, (((1,), (1,)), ((), ())), preferred_element_...  8.34 us
  transfers between devices with their start and end apart: 43, of which 15 were waited for; matrix products, arithmetic and copies ran while one was open for 35% of the time, Pallas kernels for 5%

profile of v3, /device:TPU:0, one launch (start us, length us, event | category | flops | bytes accessed | tf_op | source)
XLA Modules:
  0.0 211.9 jit_solution(26389061296754217)
XLA Ops:
  0.7 3.0 %collective-permute-start = (bf16[128,512]{1,0:T(8,128)(2,1)}, bf16[128,512]{1,0:T(8,128)(2,1)}, u32[]{:S(2)}, u32[]{:S(2)}) collective-permute-start(bf16[128,512]{1,0:T(8,128)(2,1)} %param.15), channel_id=1, source_target_pairs={{0,2},{2,0},{1,3},{3,1},{4,6},{6,4},{5,7},{7,5},{8,10},{10,8},{9,1... | collective-permute-start | bytes 393224 | tf_op jit(solution)/shard_map/ppermute | solution.py:234
  12.3 2.2 %constant_dynamic-slice_fusion.1 = (bf16[512,768]{1,0:T(8,128)(2,1)S(1)}, bf16[512,768]{1,0:T(8,128)(2,1)S(1)}, bf16[512,768]{1,0:T(8,128)(2,1)S(1)}, bf16[512,768]{1,0:T(8,128)(2,1)S(1)}) fusion(bf16[512,1536]{1,0:T(8,128)(2,1)} %param.22, s32[]{:T(128)S(6)} %select_n.216, s32[]{:T(128)S(6)} %select_n.215, bf16[512,1536]{1,0:T(8,128)(2,1)} %param.21), kind=kLoop, calls=%fused_computation.186 | loop fusion | bytes 6291464 | tf_op jit(solution)/shard_map/dynamic_slice | solution.py:301
  19.1 2.1 constant_dynamic-slice_fusion.6
  28.3 1.9 collective-permute-start.20
  31.9 4.0 %shard_map.246 = (bf16[256,512]{1,0:T(8,128)(2,1)S(1)}, f32[256,1]{1,0:T(8,128)S(1)}, f32[256,1024]{1,0:T(8,128)S(1)}, bf16[256,1024]{1,0:T(8,128)(2,1)S(1)}, bf16[256,512]{1,0:T(8,128)(2,1)S(1)}) custom-call(bf16[256,512]{1,0:T(8,128)(2,1)S(1)} %constant_dynamic-update-slice_fusion.x_own_ref, bf16[256,512]{1,0:T(8,128)(2,1)S(1)} %collective-permute-done.1.x_other_ref, ...), custom_call_target="tpu_custom_call" | custom-call | tf_op jit(solution)/shard_map/pallas_call | solution.py:52
  37.9 2.3 %convolution_add_fusion.4.act_grad_ref = f32[256,768]{1,0:T(8,128)} fusion(f32[256,768]{1,0:T(8,128)S(1)} %fusion.94, bf16[256,512]{1,0:T(8,128)(2,1)} %constant_dynamic-update-slice_fusion.2, bf16[1536,512]{1,0:T(8,128)(2,1)S(1)} %copy-done, s32[]{:T(128)S(6)} %select_n.215), kind=kOutput, calls=%fused_computation.23 | convolution fusion | flops 201523200 | bytes 2621444 | tf_op jit(solution)/shard_map/dot_general | solution.py:43
  46.9 4.6 %collective-permute-done.5 = bf16[256,512]{1,0:T(8,128)(2,1)S(1)} collective-permute-done((bf16[256,512]{1,0:T(8,128)(2,1)S(1)}, bf16[256,512]{1,0:T(8,128)(2,1)S(1)}, u32[]{:S(2)}, u32[]{:S(2)}) %collective-permute-start.5) | collective-permute-done | bytes 262176 | tf_op jit(solution)/shard_map/ppermute | solution.py:234
  53.3 2.0 copy.55
  56.8 3.4 %shard_map.247 = (bf16[256,512]{1,0:T(8,128)(2,1)S(1)}, f32[256,1]{1,0:T(8,128)S(1)}, bf16[256,768]{1,0:T(8,128)(2,1)}, bf16[256,1536]{1,0:T(8,128)(2,1)S(1)}) custom-call(f32[256,512]{1,0:T(8,128)S(1)} %get-tuple-element.75.hidden_ref, bf16[256,512]{1,0:T(8,128)(2,1)} %collective-permute-done.6.other_ref, f32[1,512]{1,0:T(1,128)S(1)} %bitcast.130, ...), custom_call_target="tpu_custom_call" | custom-call | tf_op jit(solution)/shard_map/pallas_call | solution.py:52
  83.2 4.0 %collective-permute-done.14 = bf16[256,512]{1,0:T(8,128)(2,1)S(1)} collective-permute-done((bf16[256,512]{1,0:T(8,128)(2,1)S(1)}, bf16[256,512]{1,0:T(8,128)(2,1)S(1)}, u32[]{:S(2)}, u32[]{:S(2)}) %collective-permute-start.14) | collective-permute-done | bytes 262176 | tf_op jit(solution)/shard_map/ppermute | solution.py:234
  89.1 8.8 %collective-permute-done.19 = bf16[768,256]{1,0:T(8,128)(2,1)S(1)} collective-permute-done((bf16[768,256]{1,0:T(8,128)(2,1)S(1)}, bf16[768,256]{1,0:T(8,128)(2,1)S(1)}, u32[]{:S(2)}, u32[]{:S(2)}) %collective-permute-start.19) | collective-permute-done | bytes 393248 | tf_op jit(solution)/shard_map/ppermute | solution.py:239
  111.1 6.7 %collective-permute-done.17 = bf16[256,1536]{1,0:T(8,128)(2,1)} collective-permute-done((bf16[256,1536]{1,0:T(8,128)(2,1)S(1)}, bf16[256,1536]{1,0:T(8,128)(2,1)}, u32[]{:S(2)}, u32[]{:S(2)}) %collective-permute-start.17) | collective-permute-done | bytes 786464 | tf_op jit(solution)/shard_map/ppermute | solution.py:239
  121.3 1.9 collective-permute-start.36
  129.3 3.9 %shard_map.248 = (bf16[256,1024]{1,0:T(8,128)(2,1)S(1)}, f32[1,128]{1,0:T(1,128)S(1)}, f32[1,128]{1,0:T(1,128)S(1)}) custom-call(bf16[256,512]{1,0:T(8,128)(2,1)S(1)} %get-tuple-element.44.back_own_ref, bf16[256,512]{1,0:T(8,128)(2,1)S(1)} %get-tuple-element.156.back_other_ref, bf16[512,512]{1,0:T(8,128)(2,1)S(1)} %get-tuple-element.90.output_own_ref, ...), custom_call_target="tpu_custom_call" | custom-call | tf_op jit(solution)/shard_map/pallas_call | solution.py:52
  142.2 3.2 %collective-permute-done.23 = bf16[128,512]{1,0:T(8,128)(2,1)S(1)} collective-permute-done((bf16[128,512]{1,0:T(8,128)(2,1)S(1)}, bf16[128,512]{1,0:T(8,128)(2,1)S(1)}, u32[]{:S(2)}, u32[]{:S(2)}) %collective-permute-start.23) | collective-permute-done | bytes 131104 | tf_op jit(solution)/shard_map/ppermute | solution.py:234
  145.7 2.0 collective-permute-done.26
  147.7 2.6 %collective-permute-start.37 = (bf16[192,512]{1,0:T(8,128)(2,1)S(1)}, bf16[192,512]{1,0:T(8,128)(2,1)S(1)}, u32[]{:S(2)}, u32[]{:S(2)}) collective-permute-start(bf16[192,512]{1,0:T(8,128)(2,1)S(1)} %slice.437), channel_id=1, source_target_pairs={{0,16},{4,20},{8,24},{12,28},{16,0},{20,4},{24,8},{28,12},{1,17},{... | collective-permute-start | bytes 589832 | tf_op jit(solution)/shard_map/ppermute | solution.py:239
  151.1 12.2 %collective-permute-done.32 = bf16[256,512]{1,0:T(8,128)(2,1)S(1)} collective-permute-done((bf16[256,512]{1,0:T(8,128)(2,1)S(1)}, bf16[256,512]{1,0:T(8,128)(2,1)S(1)}, u32[]{:S(2)}, u32[]{:S(2)}) %collective-permute-start.32) | collective-permute-done | bytes 262176 | tf_op jit(solution)/shard_map/ppermute | solution.py:239
  170.8 2.0 collective-permute-start.28
  175.0 16.0 %collective-permute-done.35 = bf16[64,3072]{1,0:T(8,128)(2,1)S(1)} collective-permute-done((bf16[64,3072]{1,0:T(8,128)(2,1)S(1)}, bf16[64,3072]{1,0:T(8,128)(2,1)S(1)}, u32[]{:S(2)}, u32[]{:S(2)}) %collective-permute-start.35) | collective-permute-done | bytes 393248 | tf_op jit(solution)/shard_map/ppermute | solution.py:239
  193.7 2.3 %collective-permute-done.40 = f32[10,128]{1,0:T(8,128)S(1)} collective-permute-done((f32[10,128]{1,0:T(8,128)S(1)}, f32[10,128]{1,0:T(8,128)S(1)}, u32[]{:S(2)}, u32[]{:S(2)}) %collective-permute-start.40) | collective-permute-done | bytes 5152 | tf_op jit(solution)/shard_map/ppermute | solution.py:239
  196.1 2.2 %collective-permute-start.41 = (f32[10,128]{1,0:T(8,128)S(1)}, f32[10,128]{1,0:T(8,128)S(1)}, u32[]{:S(2)}, u32[]{:S(2)}) collective-permute-start(f32[10,128]{1,0:T(8,128)S(1)} %add.248), channel_id=1, source_target_pairs={{0,16},{4,20},{8,24},{12,28},{16,0},{20,4},{24,8},{28,12},{1,17},{... | collective-permute-start | bytes 15368 | tf_op jit(solution)/shard_map/ppermute | solution.py:239
  200.0 2.2 %collective-permute-done.41 = f32[10,128]{1,0:T(8,128)S(1)} collective-permute-done((f32[10,128]{1,0:T(8,128)S(1)}, f32[10,128]{1,0:T(8,128)S(1)}, u32[]{:S(2)}, u32[]{:S(2)}) %collective-permute-start.41) | collective-permute-done | bytes 5152 | tf_op jit(solution)/shard_map/ppermute | solution.py:239
  203.9 6.4 %collective-permute-done.29 = bf16[64,2048]{1,0:T(8,128)(2,1)S(1)} collective-permute-done((bf16[64,2048]{1,0:T(8,128)(2,1)S(1)}, bf16[64,2048]{1,0:T(8,128)(2,1)S(1)}, u32[]{:S(2)}, u32[]{:S(2)}) %collective-permute-start.29) | collective-permute-done | bytes 262176 | tf_op jit(solution)/shard_map/ppermute | solution.py:239
  (346 shorter events, 107.8 us)
Async XLA Ops:
  0.7 25.3 %collective-permute-start = (bf16[128,512]{1,0:T(8,128)(2,1)}, bf16[128,512]{1,0:T(8,128)(2,1)}, u32[]{:S(2)}, u32[]{:S(2)}) collective-permute-start(bf16[128,512]{1,0:T(8,128)(2,1)} %param.15), channel_id=1, source_target_pairs={{0,2},{2,0},{1,3},{3,1},{4,6},{6,4},{5,7},{7,5},{8,10},{10,8},{9,1... | collective-permute-start | bytes 393224 | tf_op jit(solution)/shard_map/ppermute | solution.py:234
  4.4 20.2 %collective-permute-start.2 = (f32[2,512]{1,0:T(2,128)S(1)}, f32[2,512]{1,0:T(2,128)S(1)}, u32[]{:S(2)}, u32[]{:S(2)}) collective-permute-start(f32[2,512]{1,0:T(2,128)S(1)} %pad_maximum_fusion.10), channel_id=1, source_target_pairs={{0,1},{1,0},{2,3},{3,2},{4,5},{5,4},{6,7},{7,6},{8,9},{9,8},{10,11... | collective-permute-start | bytes 12296 | tf_op jit(solution)/shard_map/ppermute | solution.py:234
  8.1 23.7 %collective-permute-start.3 = (bf16[512,1024]{1,0:T(8,128)(2,1)}, bf16[512,1024]{1,0:T(8,128)(2,1)}, u32[]{:S(2)}, u32[]{:S(2)}) collective-permute-start(bf16[512,1024]{1,0:T(8,128)(2,1)} %pad_maximum_fusion.3), channel_id=1, source_target_pairs={{0,1},{1,0},{2,3},{3,2},{4,5},{5,4},{6,7},{7,6},{8,9},{9,8},{10,11... | collective-permute-start | bytes 3145736 | tf_op jit(solution)/shard_map/ppermute | solution.py:234
  8.6 13.9 %collective-permute-start.8 = (bf16[128,512]{1,0:T(8,128)(2,1)}, bf16[128,512]{1,0:T(8,128)(2,1)}, u32[]{:S(2)}, u32[]{:S(2)}) collective-permute-start(bf16[128,512]{1,0:T(8,128)(2,1)} %param.16), channel_id=1, source_target_pairs={{0,2},{2,0},{1,3},{3,1},{4,6},{6,4},{5,7},{7,5},{8,10},{10,8},{9,1... | collective-permute-start | bytes 393224 | tf_op jit(solution)/shard_map/ppermute | solution.py:234
  9.7 18.7 %collective-permute-start.10 = (bf16[768,512]{1,0:T(8,128)(2,1)}, bf16[768,512]{1,0:T(8,128)(2,1)}, u32[]{:S(2)}, u32[]{:S(2)}) collective-permute-start(bf16[768,512]{1,0:T(8,128)(2,1)} %constant_dynamic-slice_fusion), channel_id=1, source_target_pairs={{0,1},{1,0},{2,3},{3,2},{4,5},{5,4},{6,7},{7,6},{8,9},{9,8},{10,11... | collective-permute-start | bytes 2359304 | tf_op jit(solution)/shard_map/ppermute | solution.py:234
  22.4 32.9 %collective-permute-start.7 = (bf16[512,1536]{1,0:T(8,128)(2,1)}, bf16[512,1536]{1,0:T(8,128)(2,1)}, u32[]{:S(2)}, u32[]{:S(2)}) collective-permute-start(bf16[512,1536]{1,0:T(8,128)(2,1)} %pad_maximum_fusion.1), channel_id=1, source_target_pairs={{0,1},{1,0},{2,3},{3,2},{4,5},{5,4},{6,7},{7,6},{8,9},{9,8},{10,11... | collective-permute-start | bytes 4718600 | tf_op jit(solution)/shard_map/ppermute | solution.py:234
  26.0 102.2 %collective-permute-start.21 = (bf16[512,512]{1,0:T(8,128)(2,1)}, bf16[512,512]{1,0:T(8,128)(2,1)}, u32[]{:S(2)}, u32[]{:S(2)}) collective-permute-start(bf16[512,512]{1,0:T(8,128)(2,1)} %get-tuple-element.91), channel_id=1, source_target_pairs={{0,1},{1,0},{2,3},{3,2},{4,5},{5,4},{6,7},{7,6},{8,9},{9,8},{10,11... | collective-permute-start | bytes 1572872 | tf_op jit(solution)/shard_map/ppermute | solution.py:234
  28.3 71.4 %collective-permute-start.20 = (bf16[256,512]{1,0:T(8,128)(2,1)}, bf16[256,512]{1,0:T(8,128)(2,1)}, u32[]{:S(2)}, u32[]{:S(2)}) collective-permute-start(bf16[256,512]{1,0:T(8,128)(2,1)} %constant_dynamic-update-slice_fusion.2), channel_id=1, source_target_pairs={{0,4},{4,0},{8,12},{12,8},{16,20},{20,16},{24,28},{28,24},{1,5},{5... | collective-permute-start | bytes 786440 | tf_op jit(solution)/shard_map/ppermute | solution.py:239
  45.7 123.2 %collective-permute-start.25 = (bf16[256,256]{1,0:T(8,128)(2,1)}, bf16[256,256]{1,0:T(8,128)(2,1)}, u32[]{:S(2)}, u32[]{:S(2)}) collective-permute-start(bf16[256,256]{1,0:T(8,128)(2,1)} %pad_maximum_fusion.9), channel_id=1, source_target_pairs={{0,4},{4,0},{8,12},{12,8},{16,20},{20,16},{24,28},{28,24},{1,5},{5... | collective-permute-start | bytes 393224 | tf_op jit(solution)/shard_map/ppermute | solution.py:239
  64.4 70.2 %collective-permute-start.30 = (bf16[512,256]{1,0:T(8,128)(2,1)}, bf16[512,256]{1,0:T(8,128)(2,1)}, u32[]{:S(2)}, u32[]{:S(2)}) collective-permute-start(bf16[512,256]{1,0:T(8,128)(2,1)} %pad_maximum_fusion.5), channel_id=1, source_target_pairs={{0,4},{4,0},{8,12},{12,8},{16,20},{20,16},{24,28},{28,24},{1,5},{5... | collective-permute-start | bytes 786440 | tf_op jit(solution)/shard_map/ppermute | solution.py:239
  87.2 10.7 %collective-permute-start.19 = (bf16[768,256]{1,0:T(8,128)(2,1)S(1)}, bf16[768,256]{1,0:T(8,128)(2,1)S(1)}, u32[]{:S(2)}, u32[]{:S(2)}) collective-permute-start(bf16[768,256]{1,0:T(8,128)(2,1)S(1)} %pad_maximum_fusion.4), channel_id=1, source_target_pairs={{0,4},{4,0},{8,12},{12,8},{16,20},{20,16},{24,28},{28,24},{1,5},{5... | collective-permute-start | bytes 1179656 | tf_op jit(solution)/shard_map/ppermute | solution.py:239
  98.0 19.8 %collective-permute-start.17 = (bf16[256,1536]{1,0:T(8,128)(2,1)S(1)}, bf16[256,1536]{1,0:T(8,128)(2,1)}, u32[]{:S(2)}, u32[]{:S(2)}) collective-permute-start(bf16[256,1536]{1,0:T(8,128)(2,1)S(1)} %copy-done.13), channel_id=1, source_target_pairs={{0,4},{4,0},{8,12},{12,8},{16,20},{20,16},{24,28},{28,24},{1,5},{5... | collective-permute-start | bytes 2359304 | tf_op jit(solution)/shard_map/ppermute | solution.py:239
  110.8 13.8 %collective-permute-start.16 = (bf16[256,256]{1,0:T(8,128)(2,1)}, bf16[256,256]{1,0:T(8,128)(2,1)S(1)}, u32[]{:S(2)}, u32[]{:S(2)}) collective-permute-start(bf16[256,256]{1,0:T(8,128)(2,1)} %pad_maximum_fusion.8), channel_id=1, source_target_pairs={{0,4},{4,0},{8,12},{12,8},{16,20},{20,16},{24,28},{28,24},{1,5},{5... | collective-permute-start | bytes 393224 | tf_op jit(solution)/shard_map/ppermute | solution.py:239
  121.3 15.0 %collective-permute-start.36 = (bf16[384,512]{1,0:T(8,128)(2,1)S(1)}, bf16[384,512]{1,0:T(8,128)(2,1)S(1)}, u32[]{:S(2)}, u32[]{:S(2)}) collective-permute-start(bf16[384,512]{1,0:T(8,128)(2,1)S(1)} %copy-done.55), channel_id=1, source_target_pairs={{0,8},{4,12},{8,0},{12,4},{16,24},{20,28},{24,16},{28,20},{1,9},{5... | collective-permute-start | bytes 1179656 | tf_op jit(solution)/shard_map/ppermute | solution.py:239
  124.5 8.8 %collective-permute-start.31 = (bf16[256,512]{1,0:T(8,128)(2,1)S(1)}, bf16[256,512]{1,0:T(8,128)(2,1)S(1)}, u32[]{:S(2)}, u32[]{:S(2)}) collective-permute-start(bf16[256,512]{1,0:T(8,128)(2,1)S(1)} %get-tuple-element.44.back_own_ref), channel_id=1, source_target_pairs={{0,4},{4,0},{8,12},{12,8},{16,20},{20,16},{24,28},{28,24},{1,5},{5... | collective-permute-start | bytes 786440 | tf_op jit(solution)/shard_map/ppermute | solution.py:239
  133.3 14.3 %collective-permute-start.26 = (bf16[256,1024]{1,0:T(8,128)(2,1)S(1)}, bf16[256,1024]{1,0:T(8,128)(2,1)S(1)}, u32[]{:S(2)}, u32[]{:S(2)}) collective-permute-start(bf16[256,1024]{1,0:T(8,128)(2,1)S(1)} %get-tuple-element.47), channel_id=1, source_target_pairs={{0,4},{4,0},{8,12},{12,8},{16,20},{20,16},{24,28},{28,24},{1,5},{5... | collective-permute-start | bytes 1572872 | tf_op jit(solution)/shard_map/ppermute | solution.py:239
  134.5 34.1 %collective-permute-start.34 = (bf16[128,3072]{1,0:T(8,128)(2,1)S(1)}, bf16[128,3072]{1,0:T(8,128)(2,1)S(1)}, u32[]{:S(2)}, u32[]{:S(2)}) collective-permute-start(bf16[128,3072]{1,0:T(8,128)(2,1)S(1)} %slice.431), channel_id=1, source_target_pairs={{0,8},{4,12},{8,0},{12,4},{16,24},{20,28},{24,16},{28,20},{1,9},{5... | collective-permute-start | bytes 2359304 | tf_op jit(solution)/shard_map/ppermute | solution.py:239
  136.3 27.0 %collective-permute-start.32 = (bf16[256,512]{1,0:T(8,128)(2,1)S(1)}, bf16[256,512]{1,0:T(8,128)(2,1)S(1)}, u32[]{:S(2)}, u32[]{:S(2)}) collective-permute-start(bf16[256,512]{1,0:T(8,128)(2,1)S(1)} %slice.435), channel_id=1, source_target_pairs={{0,8},{4,12},{8,0},{12,4},{16,24},{20,28},{24,16},{28,20},{1,9},{5... | collective-permute-start | bytes 786440 | tf_op jit(solution)/shard_map/ppermute | solution.py:239
  147.7 17.3 %collective-permute-start.37 = (bf16[192,512]{1,0:T(8,128)(2,1)S(1)}, bf16[192,512]{1,0:T(8,128)(2,1)S(1)}, u32[]{:S(2)}, u32[]{:S(2)}) collective-permute-start(bf16[192,512]{1,0:T(8,128)(2,1)S(1)} %slice.437), channel_id=1, source_target_pairs={{0,16},{4,20},{8,24},{12,28},{16,0},{20,4},{24,8},{28,12},{1,17},{... | collective-permute-start | bytes 589832 | tf_op jit(solution)/shard_map/ppermute | solution.py:239
  150.3 18.3 %collective-permute-start.27 = (bf16[256,1024]{1,0:T(8,128)(2,1)S(1)}, bf16[256,1024]{1,0:T(8,128)(2,1)S(1)}, u32[]{:S(2)}, u32[]{:S(2)}) collective-permute-start(bf16[256,1024]{1,0:T(8,128)(2,1)S(1)} %collective-permute-done.26), channel_id=1, source_target_pairs={{0,1},{1,0},{2,3},{3,2},{4,5},{5,4},{6,7},{7,6},{8,9},{9,8},{10,11... | collective-permute-start | bytes 1572872 | tf_op jit(solution)/shard_map/ppermute | solution.py:234
  165.0 9.3 %collective-permute-start.33 = (bf16[128,512]{1,0:T(8,128)(2,1)S(1)}, bf16[128,512]{1,0:T(8,128)(2,1)S(1)}, u32[]{:S(2)}, u32[]{:S(2)}) collective-permute-start(bf16[128,512]{1,0:T(8,128)(2,1)S(1)} %slice.438), channel_id=1, source_target_pairs={{0,16},{4,20},{8,24},{12,28},{16,0},{20,4},{24,8},{28,12},{1,17},{... | collective-permute-start | bytes 393224 | tf_op jit(solution)/shard_map/ppermute | solution.py:239
  170.8 21.4 %collective-permute-start.28 = (bf16[128,2048]{1,0:T(8,128)(2,1)S(1)}, bf16[128,2048]{1,0:T(8,128)(2,1)S(1)}, u32[]{:S(2)}, u32[]{:S(2)}) collective-permute-start(bf16[128,2048]{1,0:T(8,128)(2,1)S(1)} %slice.432), channel_id=1, source_target_pairs={{0,8},{4,12},{8,0},{12,4},{16,24},{20,28},{24,16},{28,20},{1,9},{5... | collective-permute-start | bytes 1572872 | tf_op jit(solution)/shard_map/ppermute | solution.py:239
  173.0 18.0 %collective-permute-start.35 = (bf16[64,3072]{1,0:T(8,128)(2,1)S(1)}, bf16[64,3072]{1,0:T(8,128)(2,1)S(1)}, u32[]{:S(2)}, u32[]{:S(2)}) collective-permute-start(bf16[64,3072]{1,0:T(8,128)(2,1)S(1)} %slice.433), channel_id=1, source_target_pairs={{0,16},{4,20},{8,24},{12,28},{16,0},{20,4},{24,8},{28,12},{1,17},{... | collective-permute-start | bytes 1179656 | tf_op jit(solution)/shard_map/ppermute | solution.py:239
  199.3 11.1 %collective-permute-start.29 = (bf16[64,2048]{1,0:T(8,128)(2,1)S(1)}, bf16[64,2048]{1,0:T(8,128)(2,1)S(1)}, u32[]{:S(2)}, u32[]{:S(2)}) collective-permute-start(bf16[64,2048]{1,0:T(8,128)(2,1)S(1)} %slice.436), channel_id=1, source_target_pairs={{0,16},{4,20},{8,24},{12,28},{16,0},{20,4},{24,8},{28,12},{1,17},{... | collective-permute-start | bytes 786440 | tf_op jit(solution)/shard_map/ppermute | solution.py:239
  (92 other events, 410.1 us)
